TPU v7x, 32 devices: a whole 2x2x4 slice. The times are simulated.
32 devices in a mesh: dp: 8 (over z, y), tensor: 4 (over x, core).
Axes of the slice: x: 2, y: 2, z: 4, core: 2. Of those that a mesh axis runs over, the one named last changes fastest.
Arguments:
- lang_in: bfloat16 [3840, 768], P(('dp', 'tensor')), may hold values from -6 to 6
- visn_in: bfloat16 [6912, 768], P(('dp', 'tensor')), may hold values from -6 to 6
- word_len: int32 [192], P(('dp', 'tensor')), may hold values from 5 to 20, as said below
- lang_cot: bfloat16 [3840, 768], P(('dp', 'tensor')), may hold values from -6 to 6
- visn_cot: bfloat16 [6912, 768], P(('dp', 'tensor')), may hold values from -6 to 6
- att_in: float32 [3, 768, 3, 768], P(None, 'dp', None, 'tensor'), may hold values from -0.21875 to 0.21875
- att_out: float32 [3, 768, 768], P(None, 'tensor', 'dp'), may hold values from -0.875 to 0.875
- ffn_up: float32 [2, 768, 3072], P(None, 'dp', 'tensor'), may hold values from -0.21875 to 0.21875
- ffn_down: float32 [2, 3072, 768], P(None, 'tensor', 'dp'), may hold values from -0.109375 to 0.109375
- vectors: float32 [21, 768], replicated, as said below
- ffn_bias1: float32 [2, 3072], replicated, may hold values from -3 to 3
- att_in_m: float32 [3, 768, 3, 768], P(None, 'dp', None, 'tensor'), may hold values from -192 to 192
- att_in_v: float32 [3, 768, 3, 768], P(None, 'dp', None, 'tensor'), may hold values from 967.68 to 3870.72
- att_out_m: float32 [3, 768, 768], P(None, 'tensor', 'dp'), may hold values from -192 to 192
- att_out_v: float32 [3, 768, 768], P(None, 'tensor', 'dp'), may hold values from 967.68 to 3870.72
- ffn_up_m: float32 [2, 768, 3072], P(None, 'dp', 'tensor'), may hold values from -128 to 128
- ffn_up_v: float32 [2, 768, 3072], P(None, 'dp', 'tensor'), may hold values from 430.08 to 1720.32
- ffn_down_m: float32 [2, 3072, 768], P(None, 'tensor', 'dp'), may hold values from -256 to 256
- ffn_down_v: float32 [2, 3072, 768], P(None, 'tensor', 'dp'), may hold values from 1720.32 to 6881.28
- vectors_m: float32 [21, 768], replicated, may hold values from -448 to 448
- vectors_v: float32 [21, 768], replicated, may hold values from 5268.48 to 21073.92
- bias1_m: float32 [2, 3072], replicated, may hold values from -128 to 128
- bias1_v: float32 [2, 3072], replicated, may hold values from 430.08 to 1720.32
Outputs:
- lang_out: float32 [3840, 768], P(('dp', 'tensor'))
- visn_out: float32 [6912, 768], P(('dp', 'tensor'))
- lang_grad: float32 [3840, 768], P(('dp', 'tensor'))
- visn_grad: float32 [6912, 768], P(('dp', 'tensor'))
- att_in_grad: float32 [3, 768, 3, 768], P(None, 'dp', None, 'tensor')
- att_in_m_new: float32 [3, 768, 3, 768], P(None, 'dp', None, 'tensor')
- att_in_v_new: float32 [3, 768, 3, 768], P(None, 'dp', None, 'tensor')
- att_in_new: float32 [3, 768, 3, 768], P(None, 'dp', None, 'tensor')
- att_in_copy: bfloat16 [3, 768, 3, 768], P(None, 'dp', None, 'tensor')
- att_out_grad: float32 [3, 768, 768], P(None, 'tensor', 'dp')
- att_out_m_new: float32 [3, 768, 768], P(None, 'tensor', 'dp')
- att_out_v_new: float32 [3, 768, 768], P(None, 'tensor', 'dp')
- att_out_new: float32 [3, 768, 768], P(None, 'tensor', 'dp')
- att_out_copy: bfloat16 [3, 768, 768], P(None, 'tensor', 'dp')
- ffn_up_grad: float32 [2, 768, 3072], P(None, 'dp', 'tensor')
- ffn_up_m_new: float32 [2, 768, 3072], P(None, 'dp', 'tensor')
- ffn_up_v_new: float32 [2, 768, 3072], P(None, 'dp', 'tensor')
- ffn_up_new: float32 [2, 768, 3072], P(None, 'dp', 'tensor')
- ffn_up_copy: bfloat16 [2, 768, 3072], P(None, 'dp', 'tensor')
- ffn_down_grad: float32 [2, 3072, 768], P(None, 'tensor', 'dp')
- ffn_down_m_new: float32 [2, 3072, 768], P(None, 'tensor', 'dp')
- ffn_down_v_new: float32 [2, 3072, 768], P(None, 'tensor', 'dp')
- ffn_down_new: float32 [2, 3072, 768], P(None, 'tensor', 'dp')
- ffn_down_copy: bfloat16 [2, 3072, 768], P(None, 'tensor', 'dp')
- vectors_grad: float32 [21, 768], replicated
- vectors_m_new: float32 [21, 768], replicated
- vectors_v_new: float32 [21, 768], replicated
- vectors_new: float32 [21, 768], replicated
- bias1_grad: float32 [2, 3072], replicated
- bias1_m_new: float32 [2, 3072], replicated
- bias1_v_new: float32 [2, 3072], replicated
- bias1_new: float32 [2, 3072], replicated
Inputs may be any that keep to these rules, and one draw needn't show every extreme that they name: Each item has 20 word slots, of which the first word_len are words; some item has all 20. `vectors`: rows 3, 8, 13, 16 and 19 are layer norms' gains, positive; the other rows are biases and shifts.
All inputs are finite; a program needn't handle non-finite values.
Results may differ from a plain program's by a relative error of at most 0.033.
Values may be sent and summed in bfloat16 or wider, within the bound.
No kernel may reach another device: no remote copies, remote signals or barrier semaphores. Data moves between devices by JAX's collectives and lax.ppermute only.
A program may use at most 128 MiB of HBM per device.

v0:
```python
import jax
import jax.numpy as jnp
from jax import lax
from jax.sharding import PartitionSpec as P

HD = 64
FF = 3072
LW = 20
STEP = 10


lnorm_eps = 1e-12
decay_one = 0.5
decay_two = 0.5
adam_eps = 1e-08
weight_decay = 0.01
rate_in = 0.03
rate_out = 0.1
rate_up = 0.03
rate_down = 0.015
rate_vector = 0.2
rate_bias = 0.2


def layer_norm(summed, gain, shift):
    centre = jnp.mean(summed, axis=-1, keepdims=True)
    centered = summed - centre
    spread = jnp.mean(centered * centered, axis=-1, keepdims=True)
    return centered * lax.rsqrt(spread + lnorm_eps) * gain + shift


def gelu_exact(inner):
    return 0.5 * inner * (1.0 + lax.erf(inner * 0.7071067811865476))


def adam_step(weight, gradient, first, second, rate):
    first_new = decay_one * first + (1.0 - decay_one) * gradient
    second_new = decay_two * second + (1.0 - decay_two) * gradient * gradient
    fix_one = 1.0 - decay_one**STEP
    fix_two = 1.0 - decay_two**STEP
    ratio = first_new / fix_one / (jnp.sqrt(second_new / fix_two) + adam_eps)
    return (first_new, second_new, weight - rate * (ratio + weight_decay * weight))


def spread_rows(lang_part, visn_part, lengths):
    return (
        lax.all_gather(lang_part, "tensor", axis=0, tiled=True),
        lax.all_gather(visn_part, "tensor", axis=0, tiled=True),
        lax.all_gather(lengths, "tensor", axis=0, tiled=True),
    )


def collect_rows(lang_part, visn_part):
    return (
        lax.psum_scatter(
            lang_part.astype(jnp.bfloat16), "tensor", scatter_dimension=0, tiled=True
        ).astype(jnp.float32),
        lax.psum_scatter(
            visn_part.astype(jnp.bfloat16), "tensor", scatter_dimension=0, tiled=True
        ).astype(jnp.float32),
    )


def spread_grads(lang_part, visn_part):
    return (
        lax.all_gather(lang_part, "tensor", axis=0, tiled=True),
        lax.all_gather(visn_part, "tensor", axis=0, tiled=True),
    )


def collect_grads(lang_part, visn_part):
    return (
        lax.psum_scatter(
            lang_part.astype(jnp.bfloat16), "tensor", scatter_dimension=0, tiled=True
        ).astype(jnp.float32),
        lax.psum_scatter(
            visn_part.astype(jnp.bfloat16), "tensor", scatter_dimension=0, tiled=True
        ).astype(jnp.float32),
    )


def place_at(piece, start, length):
    return lax.dynamic_update_slice(jnp.zeros((length,), jnp.float32), piece, (start,))


def project(stream, w_block, bias):
    packed = jnp.dot(
        stream, w_block.reshape(w_block.shape[0], -1), preferred_element_type=jnp.float32
    )
    return (packed.reshape(stream.shape[0], 3, -1) + bias).astype(jnp.bfloat16)


def heads(packed, which, items):
    return packed[:, which].reshape(items, -1, packed.shape[2] // HD, HD)


def merge_heads(split):
    return split.reshape(-1, split.shape[2] * split.shape[3])


def scores_of(queries, key_rows, usable):
    factor = queries.shape[-1] ** (-0.5)
    scores = (
        jnp.einsum("gqhd,gkhd->ghqk", queries, key_rows, preferred_element_type=jnp.float32)
        * factor
    )
    if usable is not None:
        scores = jnp.where(usable[:, None, None, :], scores, -1e30)
    return scores


def attend(queries, key_rows, value_rows, usable):
    scores = scores_of(queries, key_rows, usable)
    maxima = jnp.max(scores, axis=-1, keepdims=True)
    powers = jnp.exp(scores - maxima)
    totals = jnp.sum(powers, axis=-1, keepdims=True)
    weights = (powers / totals).astype(jnp.bfloat16)
    mixed = jnp.einsum("ghqk,gkhd->gqhd", weights, value_rows, preferred_element_type=jnp.float32)
    return (mixed.astype(jnp.bfloat16), maxima + jnp.log(totals))


def attend_back(queries, key_rows, value_rows, usable, log_sums, grad_mixed):
    factor = queries.shape[-1] ** (-0.5)
    weights = jnp.exp(scores_of(queries, key_rows, usable) - log_sums)
    grad_values = jnp.einsum(
        "ghqk,gqhd->gkhd",
        weights.astype(jnp.bfloat16),
        grad_mixed,
        preferred_element_type=jnp.float32,
    )
    grad_weights = jnp.einsum(
        "gqhd,gkhd->ghqk", grad_mixed, value_rows, preferred_element_type=jnp.float32
    )
    grad_scores = weights * (grad_weights - jnp.sum(weights * grad_weights, axis=-1, keepdims=True))
    scaled = grad_scores.astype(jnp.bfloat16) * factor
    grad_queries = jnp.einsum(
        "ghqk,gkhd->gqhd", scaled, key_rows, preferred_element_type=jnp.float32
    )
    grad_keys = jnp.einsum("ghqk,gqhd->gkhd", scaled, queries, preferred_element_type=jnp.float32)
    return (grad_queries, grad_keys, grad_values)


def local(
    lang_in,
    visn_in,
    word_len,
    lang_cot,
    visn_cot,
    att_in,
    att_out,
    ffn_up,
    ffn_down,
    vectors,
    ffn_bias1,
    att_in_m,
    att_in_v,
    att_out_m,
    att_out_v,
    ffn_up_m,
    ffn_up_v,
    ffn_down_m,
    ffn_down_v,
    vectors_m,
    vectors_v,
    bias1_m,
    bias1_v,
):
    w_in, w_out, w_up, w_down = (
        lax.all_gather(att_in.astype(jnp.bfloat16), "dp", axis=1, tiled=True),
        lax.all_gather(att_out.astype(jnp.bfloat16), "dp", axis=2, tiled=True),
        lax.all_gather(ffn_up.astype(jnp.bfloat16), "dp", axis=1, tiled=True),
        lax.all_gather(ffn_down.astype(jnp.bfloat16), "dp", axis=2, tiled=True),
    )
    width = lang_in.shape[1]
    local_cols = w_in.shape[3]
    local_ff = w_up.shape[2]
    offset = lax.axis_index("tensor")
    col_start = offset * local_cols
    ff_start = offset * local_ff

    def head_bias(block):
        query_bias = lax.dynamic_slice_in_dim(vectors[5 * block], col_start, local_cols)
        value_bias = lax.dynamic_slice_in_dim(vectors[5 * block + 1], col_start, local_cols)
        return jnp.stack([query_bias, jnp.zeros_like(query_bias), value_bias])

    lang_rows, visn_rows, lengths = spread_rows(lang_in, visn_in, word_len)
    items = lengths.shape[0]
    usable = jnp.arange(LW, dtype=jnp.int32)[None, :] < lengths[:, None]

    def cross_forward(lang_group, visn_group):
        qkv_lang = project(lang_group, w_in[0], head_bias(0))
        qkv_visn = project(visn_group, w_in[0], head_bias(0))
        mix_lang, sums_lang = attend(
            heads(qkv_lang, 0, items), heads(qkv_visn, 1, items), heads(qkv_visn, 2, items), None
        )
        mix_visn, sums_visn = attend(
            heads(qkv_visn, 0, items), heads(qkv_lang, 1, items), heads(qkv_lang, 2, items), usable
        )
        return (qkv_lang, qkv_visn, mix_lang, mix_visn, sums_lang, sums_visn)

    cross_kept = cross_forward(lang_rows, visn_rows)
    part_lang = jnp.dot(merge_heads(cross_kept[2]), w_out[0], preferred_element_type=jnp.float32)
    part_visn = jnp.dot(merge_heads(cross_kept[3]), w_out[0], preferred_element_type=jnp.float32)
    sum_lang, sum_visn = collect_rows(part_lang, part_visn)
    lang_first_in = lang_in.astype(jnp.float32) + sum_lang + vectors[2]
    visn_first_in = visn_in.astype(jnp.float32) + sum_visn + vectors[2]
    lang_first = layer_norm(lang_first_in, vectors[3], vectors[4])
    visn_first = layer_norm(visn_first_in, vectors[3], vectors[4])

    def self_forward(stream_rows, block, mask):
        qkv = project(stream_rows, w_in[block], head_bias(block))
        mixed, log_sums = attend(
            heads(qkv, 0, items), heads(qkv, 1, items), heads(qkv, 2, items), mask
        )
        part = jnp.dot(merge_heads(mixed), w_out[block], preferred_element_type=jnp.float32)
        return (qkv, mixed, log_sums, part)

    self_lang_rows, self_visn_rows, spare = spread_rows(
        lang_first.astype(jnp.bfloat16), visn_first.astype(jnp.bfloat16), word_len
    )
    self_lang = self_forward(self_lang_rows, 1, usable)
    self_visn = self_forward(self_visn_rows, 2, None)
    sum_lang, sum_visn = collect_rows(self_lang[3], self_visn[3])
    lang_second_in = lang_first + sum_lang + vectors[7]
    visn_second_in = visn_first + sum_visn + vectors[12]
    lang_second = layer_norm(lang_second_in, vectors[8], vectors[9])
    visn_second = layer_norm(visn_second_in, vectors[13], vectors[14])

    def feed_forward(stream_rows, which):
        bias = lax.dynamic_slice_in_dim(ffn_bias1[which], ff_start, local_ff)
        inner = jnp.dot(stream_rows, w_up[which], preferred_element_type=jnp.float32) + bias
        active = gelu_exact(inner).astype(jnp.bfloat16)
        return (inner, active, jnp.dot(active, w_down[which], preferred_element_type=jnp.float32))

    feed_lang_rows, feed_visn_rows, spare = spread_rows(
        lang_second.astype(jnp.bfloat16), visn_second.astype(jnp.bfloat16), word_len
    )
    feed_lang = feed_forward(feed_lang_rows, 0)
    feed_visn = feed_forward(feed_visn_rows, 1)
    sum_lang, sum_visn = collect_rows(feed_lang[2], feed_visn[2])
    lang_third_in = lang_second + sum_lang + vectors[15]
    visn_third_in = visn_second + sum_visn + vectors[18]
    lang_out = layer_norm(lang_third_in, vectors[16], vectors[17])
    visn_out = layer_norm(visn_third_in, vectors[19], vectors[20])
    vector_rows = [jnp.zeros((width,), jnp.float32) for number in range(21)]

    def norm_back(summed, bias_row, grad_after):
        unused, back = jax.vjp(layer_norm, summed, vectors[bias_row + 1], vectors[bias_row + 2])
        grad_sum, grad_gain, grad_shift = back(grad_after)
        vector_rows[bias_row] = vector_rows[bias_row] + jnp.sum(grad_sum, axis=0)
        vector_rows[bias_row + 1] = vector_rows[bias_row + 1] + grad_gain
        vector_rows[bias_row + 2] = vector_rows[bias_row + 2] + grad_shift
        return grad_sum

    def input_back(stream_rows, grad_qkv, block):
        flat = grad_qkv.reshape(grad_qkv.shape[0], -1)
        grad_weight = jnp.einsum(
            "nd,nc->dc", stream_rows, flat, preferred_element_type=jnp.float32
        ).reshape(width, 3, local_cols)
        column_sums = jnp.sum(grad_qkv.astype(jnp.float32), axis=0)
        vector_rows[5 * block] = vector_rows[5 * block] + place_at(column_sums[0], col_start, width)
        vector_rows[5 * block + 1] = vector_rows[5 * block + 1] + place_at(
            column_sums[2], col_start, width
        )
        grad_stream = jnp.einsum(
            "nc,dc->nd", flat, w_in[block].reshape(width, -1), preferred_element_type=jnp.float32
        )
        return (grad_weight, grad_stream)

    def feed_back(stream_rows, kept, wide_grad, which):
        inner, active, unused = kept
        grad_down = jnp.einsum("nf,nd->fd", active, wide_grad, preferred_element_type=jnp.float32)
        grad_active = jnp.einsum(
            "nd,fd->nf", wide_grad, w_down[which], preferred_element_type=jnp.float32
        )
        grad_inner = jax.vjp(gelu_exact, inner)[1](grad_active)[0].astype(jnp.bfloat16)
        grad_up = jnp.einsum(
            "nd,nf->df", stream_rows, grad_inner, preferred_element_type=jnp.float32
        )
        bias_grad = jnp.sum(grad_inner.astype(jnp.float32), axis=0)
        grad_stream = jnp.einsum(
            "nf,df->nd", grad_inner, w_up[which], preferred_element_type=jnp.float32
        )
        return (grad_up, grad_down, bias_grad, grad_stream)

    grad_lang = norm_back(lang_third_in, 15, lang_cot.astype(jnp.float32))
    grad_visn = norm_back(visn_third_in, 18, visn_cot.astype(jnp.float32))
    wide_lang, wide_visn = spread_grads(
        grad_lang.astype(jnp.bfloat16), grad_visn.astype(jnp.bfloat16)
    )
    back_lang = feed_back(feed_lang_rows, feed_lang, wide_lang, 0)
    back_visn = feed_back(feed_visn_rows, feed_visn, wide_visn, 1)
    bias1_local = jnp.stack(
        [place_at(back_lang[2], ff_start, FF), place_at(back_visn[2], ff_start, FF)]
    )
    into_lang, into_visn = collect_grads(back_lang[3], back_visn[3])
    grad_lang = grad_lang + into_lang
    grad_visn = grad_visn + into_visn

    def self_back(stream_rows, kept, wide_grad, block, mask):
        qkv, mixed, log_sums, unused = kept
        grad_out = jnp.einsum(
            "nc,nd->cd", merge_heads(mixed), wide_grad, preferred_element_type=jnp.float32
        )
        grad_mixed = jnp.einsum(
            "nd,cd->nc", wide_grad, w_out[block], preferred_element_type=jnp.float32
        ).astype(jnp.bfloat16)
        grad_queries, grad_keys, grad_values = attend_back(
            heads(qkv, 0, items),
            heads(qkv, 1, items),
            heads(qkv, 2, items),
            mask,
            log_sums,
            grad_mixed.reshape(mixed.shape),
        )
        grad_qkv = jnp.stack(
            [merge_heads(grad_queries), merge_heads(grad_keys), merge_heads(grad_values)], axis=1
        ).astype(jnp.bfloat16)
        grad_weight, grad_stream = input_back(stream_rows, grad_qkv, block)
        return (grad_weight, grad_out, grad_stream)

    grad_lang = norm_back(lang_second_in, 7, grad_lang)
    grad_visn = norm_back(visn_second_in, 12, grad_visn)
    wide_lang, wide_visn = spread_grads(
        grad_lang.astype(jnp.bfloat16), grad_visn.astype(jnp.bfloat16)
    )
    self_lang_back = self_back(self_lang_rows, self_lang, wide_lang, 1, usable)
    self_visn_back = self_back(self_visn_rows, self_visn, wide_visn, 2, None)
    into_lang, into_visn = collect_grads(self_lang_back[2], self_visn_back[2])
    grad_lang = grad_lang + into_lang
    grad_visn = grad_visn + into_visn
    grad_lang = norm_back(lang_first_in, 2, grad_lang)
    grad_visn = norm_back(visn_first_in, 2, grad_visn)
    wide_lang, wide_visn = spread_grads(
        grad_lang.astype(jnp.bfloat16), grad_visn.astype(jnp.bfloat16)
    )
    again_lang, again_visn, spare = spread_rows(lang_in, visn_in, word_len)
    cross_used = cross_forward(again_lang, again_visn)
    qkv_lang, qkv_visn, mix_lang, mix_visn, sums_lang, sums_visn = cross_used
    grad_out_cross = jnp.einsum(
        "nc,nd->cd", merge_heads(mix_lang), wide_lang, preferred_element_type=jnp.float32
    ) + jnp.einsum(
        "nc,nd->cd", merge_heads(mix_visn), wide_visn, preferred_element_type=jnp.float32
    )
    mixed_lang_grad = jnp.einsum(
        "nd,cd->nc", wide_lang, w_out[0], preferred_element_type=jnp.float32
    ).astype(jnp.bfloat16)
    mixed_visn_grad = jnp.einsum(
        "nd,cd->nc", wide_visn, w_out[0], preferred_element_type=jnp.float32
    ).astype(jnp.bfloat16)
    query_lang, key_visn, value_visn = attend_back(
        heads(qkv_lang, 0, items),
        heads(qkv_visn, 1, items),
        heads(qkv_visn, 2, items),
        None,
        sums_lang,
        mixed_lang_grad.reshape(mix_lang.shape),
    )
    query_visn, key_lang, value_lang = attend_back(
        heads(qkv_visn, 0, items),
        heads(qkv_lang, 1, items),
        heads(qkv_lang, 2, items),
        usable,
        sums_visn,
        mixed_visn_grad.reshape(mix_visn.shape),
    )
    qkv_lang_grad = jnp.stack(
        [merge_heads(query_lang), merge_heads(key_lang), merge_heads(value_lang)], axis=1
    ).astype(jnp.bfloat16)
    qkv_visn_grad = jnp.stack(
        [merge_heads(query_visn), merge_heads(key_visn), merge_heads(value_visn)], axis=1
    ).astype(jnp.bfloat16)
    cross_in_lang, stream_lang = input_back(again_lang, qkv_lang_grad, 0)
    cross_in_visn, stream_visn = input_back(again_visn, qkv_visn_grad, 0)
    into_lang, into_visn = collect_grads(stream_lang, stream_visn)
    lang_grad = grad_lang + into_lang
    visn_grad = grad_visn + into_visn
    grad_in = jnp.stack([cross_in_lang + cross_in_visn, self_lang_back[0], self_visn_back[0]])
    grad_out = jnp.stack([grad_out_cross, self_lang_back[1], self_visn_back[1]])
    grad_up = jnp.stack([back_lang[0], back_visn[0]])
    grad_down = jnp.stack([back_lang[1], back_visn[1]])
    share_in, share_out, share_up, share_down = (
        lax.psum_scatter(
            grad_in.astype(jnp.bfloat16), "dp", scatter_dimension=1, tiled=True
        ).astype(jnp.float32),
        lax.psum_scatter(
            grad_out.astype(jnp.bfloat16), "dp", scatter_dimension=2, tiled=True
        ).astype(jnp.float32),
        lax.psum_scatter(
            grad_up.astype(jnp.bfloat16), "dp", scatter_dimension=1, tiled=True
        ).astype(jnp.float32),
        lax.psum_scatter(
            grad_down.astype(jnp.bfloat16), "dp", scatter_dimension=2, tiled=True
        ).astype(jnp.float32),
    )
    vector_grad, bias1_grad = lax.psum((jnp.stack(vector_rows), bias1_local), ("dp", "tensor"))
    in_first, in_second, in_new = adam_step(att_in, share_in, att_in_m, att_in_v, rate_in)
    out_first, out_second, out_new = adam_step(att_out, share_out, att_out_m, att_out_v, rate_out)
    up_first, up_second, up_new = adam_step(ffn_up, share_up, ffn_up_m, ffn_up_v, rate_up)
    down_first, down_second, down_new = adam_step(
        ffn_down, share_down, ffn_down_m, ffn_down_v, rate_down
    )
    vec_first, vec_second, vec_new = adam_step(
        vectors, vector_grad, vectors_m, vectors_v, rate_vector
    )
    bias_first, bias_second, bias_new = adam_step(
        ffn_bias1, bias1_grad, bias1_m, bias1_v, rate_bias
    )
    return (
        lang_out,
        visn_out,
        lang_grad,
        visn_grad,
        share_in,
        in_first,
        in_second,
        in_new,
        in_new.astype(jnp.bfloat16),
        share_out,
        out_first,
        out_second,
        out_new,
        out_new.astype(jnp.bfloat16),
        share_up,
        up_first,
        up_second,
        up_new,
        up_new.astype(jnp.bfloat16),
        share_down,
        down_first,
        down_second,
        down_new,
        down_new.astype(jnp.bfloat16),
        vector_grad,
        vec_first,
        vec_second,
        vec_new,
        bias1_grad,
        bias_first,
        bias_second,
        bias_new,
    )


def solution(mesh):
    return jax.shard_map(
        local,
        mesh=mesh,
        in_specs=(
            P(("dp", "tensor"), None),
            P(("dp", "tensor"), None),
            P(("dp", "tensor")),
            P(("dp", "tensor"), None),
            P(("dp", "tensor"), None),
            P(None, "dp", None, "tensor"),
            P(None, "tensor", "dp"),
            P(None, "dp", "tensor"),
            P(None, "tensor", "dp"),
            P(),
            P(),
            P(None, "dp", None, "tensor"),
            P(None, "dp", None, "tensor"),
            P(None, "tensor", "dp"),
            P(None, "tensor", "dp"),
            P(None, "dp", "tensor"),
            P(None, "dp", "tensor"),
            P(None, "tensor", "dp"),
            P(None, "tensor", "dp"),
            P(),
            P(),
            P(),
            P(),
        ),
        out_specs=(
            P(("dp", "tensor"), None),
            P(("dp", "tensor"), None),
            P(("dp", "tensor"), None),
            P(("dp", "tensor"), None),
            P(None, "dp", None, "tensor"),
            P(None, "dp", None, "tensor"),
            P(None, "dp", None, "tensor"),
            P(None, "dp", None, "tensor"),
            P(None, "dp", None, "tensor"),
            P(None, "tensor", "dp"),
            P(None, "tensor", "dp"),
            P(None, "tensor", "dp"),
            P(None, "tensor", "dp"),
            P(None, "tensor", "dp"),
            P(None, "dp", "tensor"),
            P(None, "dp", "tensor"),
            P(None, "dp", "tensor"),
            P(None, "dp", "tensor"),
            P(None, "dp", "tensor"),
            P(None, "tensor", "dp"),
            P(None, "tensor", "dp"),
            P(None, "tensor", "dp"),
            P(None, "tensor", "dp"),
            P(None, "tensor", "dp"),
            P(),
            P(),
            P(),
            P(),
            P(),
            P(),
            P(),
            P(),
        ),
        check_vma=False,
    )
```

profile of v0, /device:TPU:0, one launch (start us, length us, event | category | flops | bytes accessed | tf_op | source)
XLA Modules:
  0.0 1216.8 jit_solution(3533869772731102704)
XLA Ops:
  11.5 45.7 %all_gather.56 = bf16[3,192,768]{1,0,2:T(4,128)(2,1)S(1)} all-gather(bf16[3,192,96]{1,0,2:T(4,128)(2,1)S(1)} %copy.493), channel_id=1, replica_groups=mesh['dp'=8,'tensor'=4] {'dp'}, dimensions={2}, use_global_device_ids=true | all-gather | bytes 995328 | tf_op jit(solution)/shard_map/all_gather | solution.py:170
  67.8 8.1 all_gather.55
  75.9 31.6 %all-gather.12.cloned.1.call-done = bf16[3,768,3,192]{3,2,0,1:T(4,128)(2,1)} async-done(((bf16[3,96,3,192]{3,2,0,1:T(4,128)(2,1)}), bf16[3,768,3,192]{3,2,0,1:T(4,128)(2,1)}) %all-gather.12.cloned.1.call-update) | async-done | bytes 2654224 | tf_op jit(solution)/shard_map/all_gather | solution.py:169
  120.1 5.5 all-gather.10.cloned.1.call-done
  143.4 26.7 %reduce-scatter.26.cloned.1.call-done = bf16[216,768]{1,0:T(8,128)(2,1)} async-done(((bf16[864,768]{1,0:T(8,128)(2,1)}), bf16[216,768]{1,0:T(8,128)(2,1)}) %reduce-scatter.26.cloned.1.call-update) | async-done | bytes 331792 | tf_op jit(solution)/shard_map/reduce_scatter | solution.py:58
  178.7 13.4 %all-gather.18.cloned.1.call-done = bf16[864,768]{1,0:T(8,128)(2,1)} async-done(((bf16[216,768]{1,0:T(8,128)(2,1)}), bf16[864,768]{1,0:T(8,128)(2,1)}) %all-gather.18.cloned.1.call-update) | async-done | bytes 1327120 | tf_op jit(solution)/shard_map/all_gather | solution.py:48
  218.9 24.8 %reduce-scatter.28.cloned.1.call-done = bf16[216,768]{1,0:T(8,128)(2,1)} async-done(((bf16[864,768]{1,0:T(8,128)(2,1)}), bf16[216,768]{1,0:T(8,128)(2,1)}) %reduce-scatter.28.cloned.1.call-update) | async-done | bytes 331792 | tf_op jit(solution)/shard_map/reduce_scatter | solution.py:58
  278.9 19.6 %all-gather.14.cloned.1.call-done = bf16[2,768,768]{2,1,0:T(8,128)(2,1)} async-done(((bf16[2,96,768]{2,1,0:T(8,128)(2,1)}), bf16[2,768,768]{2,1,0:T(8,128)(2,1)}) %all-gather.14.cloned.1.call-update) | async-done | bytes 2359312 | tf_op jit(solution)/shard_map/all_gather | solution.py:171
  298.5 19.0 %all-gather.20.cloned.1.call-done = bf16[864,768]{1,0:T(8,128)(2,1)} async-done(((bf16[216,768]{1,0:T(8,128)(2,1)}), bf16[864,768]{1,0:T(8,128)(2,1)}) %all-gather.20.cloned.1.call-update) | async-done | bytes 1327120 | tf_op jit(solution)/shard_map/all_gather | solution.py:48
  322.3 50.0 %all-gather.16.cloned.1.call-done = bf16[2,768,768]{1,2,0:T(8,128)(2,1)} async-done(((bf16[2,768,96]{1,2,0:T(8,128)(2,1)}), bf16[2,768,768]{1,2,0:T(8,128)(2,1)}) %all-gather.16.cloned.1.call-update) | async-done | bytes 2359312 | tf_op jit(solution)/shard_map/all_gather | solution.py:172
  376.5 19.9 %reduce-scatter.20.cloned.1.call-done = bf16[120,768]{1,0:T(8,128)(2,1)} async-done(((bf16[480,768]{1,0:T(8,128)(2,1)}), bf16[120,768]{1,0:T(8,128)(2,1)}) %reduce-scatter.20.cloned.1.call-update) | async-done | bytes 184336 | tf_op jit(solution)/shard_map/reduce_scatter | solution.py:55
  399.9 8.3 all_gather.57
  435.2 16.7 %reduce-scatter.22.cloned.1.call-done = bf16[120,768]{1,0:T(8,128)(2,1)} async-done(((bf16[480,768]{1,0:T(8,128)(2,1)}), bf16[120,768]{1,0:T(8,128)(2,1)}) %reduce-scatter.22.cloned.1.call-update) | async-done | bytes 184336 | tf_op jit(solution)/shard_map/reduce_scatter | solution.py:55
  455.0 7.9 all_gather.59
  472.3 5.3 convert_reduce_fusion
  481.1 16.9 %reduce-scatter.24.cloned.1.call-done = bf16[120,768]{1,0:T(8,128)(2,1)} async-done(((bf16[480,768]{1,0:T(8,128)(2,1)}), bf16[120,768]{1,0:T(8,128)(2,1)}) %reduce-scatter.24.cloned.1.call-update) | async-done | bytes 184336 | tf_op jit(solution)/shard_map/reduce_scatter | solution.py:55
  503.2 8.1 all_gather.64
  515.7 11.4 reduce-scatter.36.cloned.1.call-done
  534.6 18.1 %reduce-scatter.32.cloned.1.call-done = bf16[120,768]{1,0:T(8,128)(2,1)} async-done(((bf16[480,768]{1,0:T(8,128)(2,1)}), bf16[120,768]{1,0:T(8,128)(2,1)}) %reduce-scatter.32.cloned.1.call-update) | async-done | bytes 184336 | tf_op jit(solution)/shard_map/reduce_scatter | solution.py:73
  555.6 17.4 %all-gather.24.cloned.1.call-done = bf16[864,768]{1,0:T(8,128)(2,1)} async-done(((bf16[216,768]{1,0:T(8,128)(2,1)}), bf16[864,768]{1,0:T(8,128)(2,1)}) %all-gather.24.cloned.1.call-update) | async-done | bytes 1327120 | tf_op jit(solution)/shard_map/all_gather | solution.py:67
  610.6 8.5 all_gather.65
  670.0 11.6 all_gather.66
  685.7 11.1 convolution_bitcast_fusion.8
  705.6 12.5 %convolution_bitcast_fusion.1 = bf16[24,36,3,64]{3,1,2,0:T(8,128)(2,1)} fusion(f32[24,3,20,36]{3,2,1,0:T(8,128)} %fusion.131, f32[24,3,20,36]{3,2,1,0:T(8,128)S(1)} %copy-done.10, f32[24,3,20]{2,1,0:T(4,128)S(1)} %copy-done.84, bf16[24,20,3,64]{3,2,1,0:T(4,128)(2,1)} %reshape_squeeze.32), kind=kOutput, calls=%fused_computation.43 | convolution fusion | flops 7155395 | bytes 936576 | tf_op jit(solution)/shard_map/ghqk,gqhd->gkhd/dot_general | solution.py:139
  784.7 5.9 copy.579
  790.6 9.4 reshape.524
  808.9 61.4 %reduce-scatter.44.cloned.1.call-done = bf16[2,96,768]{2,1,0:T(8,128)(2,1)} async-done(((bf16[2,768,768]{2,1,0:T(8,128)(2,1)}), bf16[2,96,768]{2,1,0:T(8,128)(2,1)}) %reduce-scatter.44.cloned.1.call-update) | async-done | bytes 294928 | tf_op jit(solution)/shard_map/reduce_scatter | solution.py:389
  873.4 124.2 %all-reduce.8.cloned.1.call-done = (f32[21,768]{1,0:T(8,128)}, f32[2,3072]{1,0:T(2,128)}) async-done(((f32[21,768]{1,0:T(8,128)}, f32[2,3072]{1,0:T(2,128)}), (f32[21,768]{1,0:T(8,128)}, f32[2,3072]{1,0:T(2,128)})) %all-reduce.8.cloned.1.call-update) | async-done | bytes 89104 | tf_op jit(solution)/shard_map/psum | solution.py:396
  1000.6 24.1 %reduce-scatter.40.cloned.1.call-done = bf16[120,768]{1,0:T(8,128)(2,1)} async-done(((bf16[480,768]{1,0:T(8,128)(2,1)}), bf16[120,768]{1,0:T(8,128)(2,1)}) %reduce-scatter.40.cloned.1.call-update) | async-done | bytes 184336 | tf_op jit(solution)/shard_map/reduce_scatter | solution.py:73
  1026.5 64.8 %reduce-scatter.48.cloned.1.call-done = bf16[96,576]{1,0:T(8,128)(2,1)} async-done(((bf16[768,576]{1,0:T(8,128)(2,1)}), bf16[96,576]{1,0:T(8,128)(2,1)}) %reduce-scatter.48.cloned.1.call-update) | async-done | bytes 110608
  1095.5 24.3 %reduce-scatter.42.cloned.1.call-done = bf16[216,768]{1,0:T(8,128)(2,1)} async-done(((bf16[864,768]{1,0:T(8,128)(2,1)}), bf16[216,768]{1,0:T(8,128)(2,1)}) %reduce-scatter.42.cloned.1.call-update) | async-done | bytes 331792 | tf_op jit(solution)/shard_map/reduce_scatter | solution.py:76
  1121.7 72.6 %reduce-scatter.46.cloned.1.call-done = bf16[96,1728]{1,0:T(8,128)(2,1)} async-done(((bf16[768,1728]{1,0:T(8,128)(2,1)}), bf16[96,1728]{1,0:T(8,128)(2,1)}) %reduce-scatter.46.cloned.1.call-update) | async-done | bytes 331792
  (773 shorter events, 393.3 us)
Async XLA Ops:
  7.2 100.3 %all-gather.12.cloned.1.call-start = ((), (), s32[]{:S(2)}) async-start(), calls=%async_computation.16 | async-start | bytes 5308416 | tf_op jit(solution)/shard_map/all_gather | solution.py:169
  9.8 115.9 %all-gather.10.cloned.1.call-start = ((), (), s32[]{:S(2)}) async-start(), calls=%async_computation.15 | async-start | bytes 1658880 | tf_op jit(solution)/shard_map/all_gather | solution.py:48
  10.5 159.6 %reduce-scatter.26.cloned.1.call-start = ((), (), s32[]{:S(2)}) async-start(), calls=%async_computation.22 | async-start | bytes 1658880 | tf_op jit(solution)/shard_map/reduce_scatter | solution.py:58
  11.3 387.5 %copy-start.71 = (f32[768]{0:T(1024)}, f32[768]{0:T(1024)S(1)}, u32[]{:S(2)}) copy-start(f32[768]{0:T(1024)S(1)} %get-tuple-element.344) | copy-start | bytes 9220
  11.3 387.5 %copy-start.89 = (f32[768]{0:T(1024)}, f32[768]{0:T(1024)S(1)}, u32[]{:S(2)}) copy-start(f32[768]{0:T(1024)S(1)} %get-tuple-element.345) | copy-start | bytes 9220
  11.3 417.1 %copy-start.87 = (f32[768]{0:T(1024)}, f32[768]{0:T(1024)S(1)}, u32[]{:S(2)}) copy-start(f32[768]{0:T(1024)S(1)} %get-tuple-element.353) | copy-start | bytes 9220
  60.3 210.0 %copy-start.20 = (bf16[1,192,768]{2,1,0:T(8,128)(2,1)}, bf16[1,192,768]{2,1,0:T(8,128)(2,1)S(1)}, u32[]{:S(2)}) copy-start(bf16[1,192,768]{2,1,0:T(8,128)(2,1)S(1)} %copy.600) | copy-start | bytes 884740
  143.4 48.7 %all-gather.18.cloned.1.call-start = ((), (), s32[]{:S(2)}) async-start(), calls=%async_computation.23 | async-start | bytes 1658880 | tf_op jit(solution)/shard_map/all_gather | solution.py:48
  173.6 70.1 %reduce-scatter.28.cloned.1.call-start = ((), (), s32[]{:S(2)}) async-start(), calls=%async_computation.24 | async-start | bytes 1658880 | tf_op jit(solution)/shard_map/reduce_scatter | solution.py:58
  217.0 81.5 %all-gather.14.cloned.1.call-start = ((), (), s32[]{:S(2)}) async-start(), calls=%async_computation.19 | async-start | bytes 2654208 | tf_op jit(solution)/shard_map/all_gather | solution.py:171
  218.9 98.6 %all-gather.20.cloned.1.call-start = ((), (), s32[]{:S(2)}) async-start(), calls=%async_computation.25 | async-start | bytes 1658880 | tf_op jit(solution)/shard_map/all_gather | solution.py:48
  246.3 126.0 %all-gather.16.cloned.1.call-start = ((), (), s32[]{:S(2)}) async-start(), calls=%async_computation.20 | async-start | bytes 2654208 | tf_op jit(solution)/shard_map/all_gather | solution.py:172
  248.2 148.2 %reduce-scatter.20.cloned.1.call-start = ((), (), s32[]{:S(2)}) async-start(), calls=%async_computation.17 | async-start | bytes 921600 | tf_op jit(solution)/shard_map/reduce_scatter | solution.py:55
  272.5 155.9 %reduce-scatter.30.cloned.1.call-start = ((), (), s32[]{:S(2)}) async-start(), calls=%async_computation.26 | async-start | bytes 1658880 | tf_op jit(solution)/shard_map/reduce_scatter | solution.py:58
  376.4 75.5 %reduce-scatter.22.cloned.1.call-start = ((), (), s32[]{:S(2)}) async-start(), calls=%async_computation.18 | async-start | bytes 921600 | tf_op jit(solution)/shard_map/reduce_scatter | solution.py:55
  428.4 44.0 %all-gather.22.cloned.1.call-start = ((), (), s32[]{:S(2)}) async-start(), calls=%async_computation.29 | async-start | bytes 1658880 | tf_op jit(solution)/shard_map/all_gather | solution.py:67
  433.9 64.2 %reduce-scatter.24.cloned.1.call-start = ((), (), s32[]{:S(2)}) async-start(), calls=%async_computation.21 | async-start | bytes 921600 | tf_op jit(solution)/shard_map/reduce_scatter | solution.py:55
  467.5 59.6 %reduce-scatter.36.cloned.1.call-start = ((), (), s32[]{:S(2)}) async-start(), calls=%async_computation.30 | async-start | bytes 1658880 | tf_op jit(solution)/shard_map/reduce_scatter | solution.py:76
  481.0 71.6 %reduce-scatter.32.cloned.1.call-start = ((), (), s32[]{:S(2)}) async-start(), calls=%async_computation.27 | async-start | bytes 921600 | tf_op jit(solution)/shard_map/reduce_scatter | solution.py:73
  515.6 57.3 %all-gather.24.cloned.1.call-start = ((), (), s32[]{:S(2)}) async-start(), calls=%async_computation.31 | async-start | bytes 1658880 | tf_op jit(solution)/shard_map/all_gather | solution.py:67
  531.6 107.0 %reduce-scatter.38.cloned.1.call-start = ((), (), s32[]{:S(2)}) async-start(), calls=%async_computation.32 | async-start | bytes 1658880 | tf_op jit(solution)/shard_map/reduce_scatter | solution.py:76
  609.9 52.9 %reduce-scatter.34.cloned.1.call-start = ((), (), s32[]{:S(2)}) async-start(), calls=%async_computation.28 | async-start | bytes 921600 | tf_op jit(solution)/shard_map/reduce_scatter | solution.py:73
  638.6 88.0 %all-gather.26.cloned.1.call-start = ((), (), s32[]{:S(2)}) async-start(), calls=%async_computation.33 | async-start | bytes 1658880 | tf_op jit(solution)/shard_map/all_gather | solution.py:67
  642.3 162.5 %all-reduce.6.cloned.1.call-start = ((), (), s32[]{:S(2)}) async-start(), calls=%async_computation.39 | async-start | bytes 4718592
  652.2 218.1 %reduce-scatter.44.cloned.1.call-start = ((), (), s32[]{:S(2)}) async-start(), calls=%async_computation.36 | async-start | bytes 2654208 | tf_op jit(solution)/shard_map/reduce_scatter | solution.py:389
  670.0 327.6 %all-reduce.8.cloned.1.call-start = ((), (), s32[]{:S(2)}) async-start(), calls=%async_computation.40 | async-start | bytes 196608 | tf_op jit(solution)/shard_map/psum | solution.py:396
  763.1 261.6 %reduce-scatter.40.cloned.1.call-start = ((), (), s32[]{:S(2)}) async-start(), calls=%async_computation.34 | async-start | bytes 921600 | tf_op jit(solution)/shard_map/reduce_scatter | solution.py:73
  766.0 325.3 %reduce-scatter.48.cloned.1.call-start = ((), (), s32[]{:S(2)}) async-start(), calls=%async_computation.38 | async-start | bytes 1105920
  773.7 346.0 %reduce-scatter.42.cloned.1.call-start = ((), (), s32[]{:S(2)}) async-start(), calls=%async_computation.35 | async-start | bytes 1658880 | tf_op jit(solution)/shard_map/reduce_scatter | solution.py:76
  778.7 415.6 %reduce-scatter.46.cloned.1.call-start = ((), (), s32[]{:S(2)}) async-start(), calls=%async_computation.37 | async-start | bytes 3096576
  808.9 215.8 %copy-start.31 = (f32[120,768]{1,0:T(8,128)S(1)}, f32[120,768]{1,0:T(8,128)}, u32[]{:S(2)}) copy-start(f32[120,768]{1,0:T(8,128)} %copy-done.30) | copy-start | bytes 1105924
  808.9 215.8 %copy-start.182 = (f32[120]{0:T(128)S(1)}, f32[120]{0:T(128)}, u32[]{:S(2)}) copy-start(f32[120]{0:T(128)} %copy-done.181) | copy-start | bytes 1444
  (199 other events, 2878.6 us)
Sparse Core Ops, SparseCore 0:
  10.8 96.6 all-gather.11
  109.1 16.4 all-gather.9
  143.5 26.6 reduce-scatter.25
  173.8 18.2 all-gather.17
  217.1 26.6 reduce-scatter.27
  246.4 52.0 all-gather.13
  300.6 16.7 all-gather.19
  320.2 52.0 all-gather.15
  374.9 21.4 reduce-scatter.19
  399.0 26.6 reduce-scatter.29
  428.5 23.4 reduce-scatter.21
  454.0 18.2 all-gather.21
  475.0 22.9 reduce-scatter.23
  500.4 26.6 reduce-scatter.35
  529.6 22.9 reduce-scatter.31
  554.7 18.2 all-gather.23
  610.0 26.6 reduce-scatter.37
  639.9 22.9 reduce-scatter.33
  665.0 20.6 all-gather.25
  689.1 109.1 all-reduce.5
  802.2 68.0 reduce-scatter.43
  877.4 120.0 all-reduce.7
  1000.9 23.8 reduce-scatter.39
  1027.9 63.3 reduce-scatter.47
  1094.0 25.6 reduce-scatter.41
  1123.1 71.1 reduce-scatter.45
where the time goes:
time: 1230 us; the launch traced here: 1220 us
  waiting for transfers between devices  671 us (55%)
  local copies, waits for them, and re-layouts  205 us (17%)
  matrix products  143 us (12%)
  blocking collectives  103 us (8%)
  other arithmetic  74.2 us (6%)
  between operations  18.6 us (2%)
    unnamed x29, waiting for transfers between devices  139 us
    psum x1, waiting for transfers between devices, local(): lax.psum((jnp.stack(vector_rows), bias1_local), ('dp', 'tensor'))  124 us
    unnamed x439, local copies, waits for them, and re-layouts  66.7 us
    reduce_scatter x1, waiting for transfers between devices, local(): lax.psum_scatter(grad_up.astype(jnp.bfloat16), 'dp', scatter_dimension=1,...  61.4 us
    reduce_scatter x3, waiting for transfers between devices, collect_rows(): lax.psum_scatter(lang_part.astype(jnp.bfloat16), 'tensor', scatter_dimens...  53.6 us
    reduce_scatter x3, waiting for transfers between devices, collect_rows(): lax.psum_scatter(visn_part.astype(jnp.bfloat16), 'tensor', scatter_dimens...  51.6 us
    all_gather x1, waiting for transfers between devices, local(): lax.all_gather(ffn_down.astype(jnp.bfloat16), 'dp', axis=2, tiled=True)  50 us
    all_gather x1, blocking collectives, local(): lax.all_gather(att_out.astype(jnp.bfloat16), 'dp', axis=2, tiled=True)  45.7 us
  transfers between devices with their start and end apart: 26, of which 22 were waited for; matrix products, arithmetic and copies ran while one was open for 25% of the time, Pallas kernels for 0%

commit v1 on v0

v1 whole, which is shorter than its diff:
```python
import functools

import jax
import jax.numpy as jnp
from jax import lax
from jax.experimental import pallas as pl
from jax.experimental.pallas import tpu as pltpu
from jax.sharding import PartitionSpec as P

HD = 64
LW = 20
STEP = 10

lnorm_eps = 1e-12
decay_one = 0.5
decay_two = 0.5
adam_eps = 1e-08
weight_decay = 0.01
rate_in = 0.03
rate_out = 0.1
rate_up = 0.03
rate_down = 0.015
rate_vector = 0.2
rate_bias = 0.2

F32 = jnp.float32
BF16 = jnp.bfloat16
HIGHEST = lax.Precision.HIGHEST

DIGITS = {
    (8, 4): {"z": ("dp", 4, 2), "y": ("dp", 2, 1), "x": ("tensor", 2, 2), "c": ("tensor", 2, 1)},
    (32, 4): {"y": ("dp", 4, 8), "z": ("dp", 4, 2), "c": ("dp", 2, 1), "x": ("tensor", 4, 1)},
}


class Tree:
    def __init__(self, mesh):
        self.sizes = dict(mesh.shape)
        shape = (self.sizes["dp"], self.sizes["tensor"])
        self.digits = DIGITS.get(shape) or {
            "z": ("dp", shape[0], 1), "x": ("tensor", shape[1], 1)
        }
        self.row_names = [n for n in ("c", "y", "z") if n in self.digits and self.digits[n][0] == "dp"]
        self.col_names = [n for n in ("x", "c") if n in self.digits and self.digits[n][0] == "tensor"]

    def order(self, text):
        return [n for n in text if n in self.digits]

    def swap(self, value, name, mask):
        axis, size, stride = self.digits[name]
        perm = [(i, i ^ (mask * stride)) for i in range(self.sizes[axis])]
        return lax.ppermute(value, axis, perm)

    def row_code(self):
        codes = [0]
        for name in self.row_names:
            axis, size, stride = self.digits[name]
            codes = [c ^ (m * stride) for c in codes for m in range(size)]
        return codes

    def gather(self, shard, text):
        state = {0: shard.reshape((1,) * len(self.row_names) + shard.shape)}
        for name in self.order(text):
            axis, size, stride = self.digits[name]
            if axis == "dp":
                at = self.row_names.index(name)
                state = {
                    j: jnp.concatenate([v] + [self.swap(v, name, m) for m in range(1, size)], axis=at)
                    for j, v in state.items()
                }
            else:
                new = dict(state)
                for j, v in state.items():
                    for m in range(1, size):
                        new[j ^ (m * stride)] = self.swap(v, name, m)
                state = new
        return [state[j].reshape(-1, shard.shape[1]) for j in range(self.sizes["tensor"])]

    def scatter(self, pieces, text):
        dims = [self.digits[n][1] for n in self.row_names]
        width = pieces[0].shape[1]
        state = {j: v.reshape(dims + [-1, width]) for j, v in enumerate(pieces)}
        for name in reversed(self.order(text)):
            axis, size, stride = self.digits[name]
            new = {}
            if axis == "dp":
                at = self.row_names.index(name)
                for j, v in state.items():
                    total = lax.slice_in_dim(v, 0, 1, axis=at).astype(F32)
                    for m in range(1, size):
                        total = total + self.swap(lax.slice_in_dim(v, m, m + 1, axis=at), name, m).astype(F32)
                    new[j] = total.astype(BF16)
            else:
                for j in [j for j in state if (j // stride) % size == 0]:
                    total = state[j].astype(F32)
                    for m in range(1, size):
                        total = total + self.swap(state[j ^ (m * stride)], name, m).astype(F32)
                    new[j] = total.astype(BF16)
            state = new
        return state[0].reshape(-1, width)

    def total(self, value):
        for name in self.order("czyx"):
            axis, size, stride = self.digits[name]
            value = sum([self.swap(value, name, m) for m in range(1, size)], value)
        return value


def adam_step(weight, gradient, first, second, rate):
    first_new = decay_one * first + (1.0 - decay_one) * gradient
    second_new = decay_two * second + (1.0 - decay_two) * gradient * gradient
    fix_one = 1.0 - decay_one**STEP
    fix_two = 1.0 - decay_two**STEP
    ratio = first_new / fix_one / (jnp.sqrt(second_new / fix_two) + adam_eps)
    return (first_new, second_new, weight - rate * (ratio + weight_decay * weight))


def mm(left, right):
    return jnp.dot(left, right, preferred_element_type=F32)


def mm_nt(left, right):
    return lax.dot_general(left, right, (((1,), (1,)), ((), ())), preferred_element_type=F32)


def mm_tn(left, right):
    return lax.dot_general(left, right, (((0,), (0,)), ((), ())), preferred_element_type=F32)


def normed(z, gain, shift):
    centered = z - jnp.mean(z, axis=-1, keepdims=True)
    scale = lax.rsqrt(jnp.mean(centered * centered, axis=-1, keepdims=True) + lnorm_eps)
    xhat = centered * scale
    return xhat * gain + shift, xhat, scale


def norm_back(g, xhat, scale, gain, sums_ref):
    gg = g * gain
    g_z = (gg - jnp.mean(gg, axis=-1, keepdims=True) - xhat * jnp.mean(gg * xhat, axis=-1, keepdims=True)) * scale
    sums_ref[...] = jnp.zeros(sums_ref.shape, F32)
    sums_ref[0:1, :] = jnp.sum(g_z, axis=0, keepdims=True)
    sums_ref[1:2, :] = jnp.sum(g * xhat, axis=0, keepdims=True)
    sums_ref[2:3, :] = jnp.sum(g, axis=0, keepdims=True)
    return g_z


def probabilities(q, k, mask):
    s = jnp.where(mask > 0, mm_nt(q, k) * HD ** (-0.5), -1e30)
    e = jnp.exp(s - jnp.max(s, axis=-1, keepdims=True))
    return e / jnp.sum(e, axis=-1, keepdims=True)


def att_fwd_kernel(n, hn, x_ref, mask_ref, bias_ref, vec_ref, *refs):
    w, (out_ref, xhat_ref, scale_ref, qkv_ref, mix_ref) = refs[:n], refs[n:]
    c = hn * HD
    x = x_ref[...]
    x16 = x.astype(BF16)
    z = x + vec_ref[0:1, :]
    rows = x.shape[0]
    lead = mix_ref.shape[2] - c
    for j in range(n):
        qkv = (mm(x16, w[j][...]) + bias_ref[j : j + 1, :]).astype(BF16)
        qkv_ref[j] = qkv
        parts = [jnp.zeros((rows, lead), BF16)]
        for h in range(hn):
            q, k, v = (qkv[:, i * c + h * HD : i * c + (h + 1) * HD] for i in range(3))
            p = probabilities(q, k, mask_ref[...]).astype(BF16)
            parts.append(mm(p, v).astype(BF16))
        mix = jnp.concatenate(parts, axis=1)
        mix_ref[j] = mix
        z = z + mm_nt(mix, w[j][:, 3 * c - lead :])
    out, xhat, scale = normed(z, vec_ref[1:2, :], vec_ref[2:3, :])
    out_ref[...] = out
    xhat_ref[...] = xhat
    scale_ref[...] = jnp.broadcast_to(scale, scale_ref.shape)


def att_bwd_kernel(n, hn, g_ref, x_ref, mask_ref, vec_ref, xhat_ref, scale_ref, qkv_ref, mix_ref, *refs):
    w, (gin_ref, sums_ref, bias_ref), dw = refs[:n], refs[n : n + 3], refs[n + 3 :]
    c = hn * HD
    x16 = x_ref[...].astype(BF16)
    g_z = norm_back(g_ref[...], xhat_ref[...], scale_ref[:, 0:1], vec_ref[1:2, :], sums_ref)
    wide = g_z.astype(BF16)
    rows = g_z.shape[0]
    lead = mix_ref.shape[2] - c
    gin = g_z
    for j in range(n):
        qkv = qkv_ref[j]
        d_mix = mm(wide, w[j][:, 3 * c - lead :]).astype(BF16)
        dq, dk, dv = [], [], []
        for h in range(hn):
            q, k, v = (qkv[:, i * c + h * HD : i * c + (h + 1) * HD] for i in range(3))
            da = d_mix[:, lead + h * HD : lead + (h + 1) * HD]
            p = probabilities(q, k, mask_ref[...])
            dv.append(mm_tn(p.astype(BF16), da).astype(BF16))
            dp = mm_nt(da, v)
            ds = (p * (dp - jnp.sum(p * dp, axis=-1, keepdims=True))).astype(BF16) * HD ** (-0.5)
            dq.append(mm(ds, k).astype(BF16))
            dk.append(mm_tn(ds, q).astype(BF16))
        d_qkv = jnp.concatenate(dq + dk + dv + [jnp.zeros((rows, c), BF16)], axis=1)
        bias_ref[j : j + 1, :] = jnp.sum(d_qkv.astype(F32), axis=0, keepdims=True)
        at = 3 * c - lead
        d_in = mm_tn(x16, d_qkv)
        dw[j][:, :at] = d_in[:, :at].astype(BF16)
        dw[j][:, at:] = (d_in[:, at:] + mm_tn(wide, mix_ref[j])).astype(BF16)
        gin = gin + mm_nt(d_qkv, w[j][...])
    gin_ref[...] = gin


def ffn_fwd_kernel(n, x_ref, cot_ref, bias_ref, vec_ref, *refs):
    up, down = refs[:n], refs[n : 2 * n]
    out_ref, gz_ref, sums_ref, act_ref, slope_ref = refs[2 * n :]
    x = x_ref[...]
    x16 = x.astype(BF16)
    z = x + vec_ref[0:1, :]
    for j in range(n):
        inner = mm(x16, up[j][...]) + bias_ref[j : j + 1, :]
        half = 0.5 * (1.0 + lax.erf(inner * 0.7071067811865476))
        act = (inner * half).astype(BF16)
        slope_ref[j] = half + inner * (0.3989422804014327 * jnp.exp(-0.5 * inner * inner))
        act_ref[j] = act
        z = z + mm_nt(act, down[j][...])
    out, xhat, scale = normed(z, vec_ref[1:2, :], vec_ref[2:3, :])
    out_ref[...] = out
    gz_ref[...] = norm_back(cot_ref[...].astype(F32), xhat, scale, vec_ref[1:2, :], sums_ref)


def ffn_down_kernel(n, gz_ref, act_ref, slope_ref, *refs):
    down, (inner_ref, bias_ref), dw = refs[:n], refs[n : n + 2], refs[n + 2 :]
    wide = gz_ref[...].astype(BF16)
    for j in range(n):
        dw[j][...] = mm_tn(wide, act_ref[j]).astype(BF16)
        d_inner = (mm(wide, down[j][...]) * slope_ref[j]).astype(BF16)
        inner_ref[j] = d_inner
        bias_ref[j : j + 1, :] = jnp.sum(d_inner.astype(F32), axis=0, keepdims=True)


def ffn_up_kernel(n, gz_ref, x_ref, inner_ref, *refs):
    up, (gin_ref,), dw = refs[:n], refs[n : n + 1], refs[n + 1 :]
    x16 = x_ref[...].astype(BF16)
    gin = gz_ref[...]
    for j in range(n):
        d_inner = inner_ref[j]
        dw[j][...] = mm_tn(x16, d_inner).astype(BF16)
        gin = gin + mm_nt(d_inner, up[j][...])
    gin_ref[...] = gin


def call(kernel, args, outs, flops):
    vmem = pl.BlockSpec(memory_space=pltpu.VMEM)
    moved = sum(a.size * a.dtype.itemsize for a in args) + sum(o.size * o.dtype.itemsize for o in outs)
    return pl.pallas_call(
        kernel,
        out_shape=tuple(outs),
        in_specs=[vmem] * len(args),
        out_specs=tuple([vmem] * len(outs)),
        compiler_params=pltpu.CompilerParams(vmem_limit_bytes=52 * 1024 * 1024),
        cost_estimate=pl.CostEstimate(flops=int(flops), bytes_accessed=int(moved), transcendentals=0),
    )(*args)


def shape(dims, kind=F32):
    return jax.ShapeDtypeStruct(dims, kind)


def att_forward(x, mask, bias, vec, w, hn):
    n, (rows, width) = len(w), x.shape
    mixed = -(-hn * HD // 256) * 256
    outs = [shape((rows, width)), shape((rows, width)), shape((rows, 128)), shape((n, rows, w[0].shape[1]), BF16), shape((n, rows, mixed), BF16)]
    return call(functools.partial(att_fwd_kernel, n, hn), [x, mask, bias, vec] + list(w), outs, 2 * rows * width * width * 4)


def att_backward(g, x, mask, vec, kept, w, hn):
    n, (rows, width) = len(w), x.shape
    outs = [shape((rows, width)), shape((8, width)), shape((n, w[0].shape[1]))] + [shape(w[0].shape, BF16)] * n
    res = call(functools.partial(att_bwd_kernel, n, hn), [g, x, mask, vec] + list(kept) + list(w), outs, 4 * rows * width * width * 4)
    return res[0], res[1], res[2], res[3:]


def ffn_forward(x, cot, bias, vec, up, down):
    n, (rows, width), f = len(up), x.shape, up[0].shape[1]
    outs = [shape((rows, width)), shape((rows, width)), shape((8, width)), shape((n, rows, f), BF16), shape((n, rows, f))]
    return call(functools.partial(ffn_fwd_kernel, n), [x, cot, bias, vec] + list(up) + list(down), outs, 4 * rows * width * f * n)


def ffn_down_back(gz, act, slope, down):
    n, (rows, width), f = len(down), gz.shape, down[0].shape[1]
    outs = [shape((n, rows, f), BF16), shape((n, f))] + [shape(down[0].shape, BF16)] * n
    res = call(functools.partial(ffn_down_kernel, n), [gz, act, slope] + list(down), outs, 4 * rows * width * f * n)
    return res[0], res[1], res[2:]


def ffn_up_back(gz, x, inner, up):
    n, (rows, width), f = len(up), gz.shape, up[0].shape[1]
    outs = [shape((rows, width))] + [shape(up[0].shape, BF16)] * n
    res = call(functools.partial(ffn_up_kernel, n), [gz, x, inner] + list(up), outs, 4 * rows * width * f * n)
    return res[0], res[1:]


def make_local(mesh):
    tree = Tree(mesh)
    n_t = mesh.shape["tensor"]
    orders = {"a0": "zyxc", "a1": "zxyc", "a2": "zyxc", "u0": "zxyc", "d0": "zyxc", "u1": "zxyc", "d1": "xyzc"}

    def local(
        lang_in, visn_in, word_len, lang_cot, visn_cot, att_in, att_out, ffn_up, ffn_down, vectors, ffn_bias1,
        att_in_m, att_in_v, att_out_m, att_out_v, ffn_up_m, ffn_up_v, ffn_down_m, ffn_down_v,
        vectors_m, vectors_v, bias1_m, bias1_v,
    ):
        width = lang_in.shape[1]
        rows = att_in.shape[1]
        cols = att_in.shape[3]
        ff = ffn_up.shape[2]
        heads_here = cols // HD
        items = word_len.shape[0]
        usable = jnp.arange(LW, dtype=jnp.int32)[None, :] < word_len[:, None]
        dp_at, t_at = lax.axis_index("dp"), lax.axis_index("tensor")

        shards = {}
        for b in range(3):
            shards["a%d" % b] = jnp.concatenate(
                [att_in[b].astype(BF16).reshape(rows, 3 * cols), att_out[b].astype(BF16).T], axis=1
            )
        for i in range(2):
            shards["u%d" % i] = ffn_up[i].astype(BF16)
            shards["d%d" % i] = ffn_down[i].astype(BF16).T
        full = {k: tree.gather(v, orders[k]) for k, v in shards.items()}

        blocks = jnp.asarray(tree.row_code(), jnp.int32) ^ dp_at
        index_of = (blocks[:, None] * rows + jnp.arange(rows, dtype=jnp.int32)[None, :]).reshape(-1)
        turn = (jnp.arange(width, dtype=jnp.int32)[:, None] == index_of[None, :])
        turn16, turn32 = turn.astype(BF16), turn.astype(F32)

        def to_rel(value):
            return mm(value, turn16).astype(BF16)

        def to_abs(value):
            return lax.dot_general(value, turn32, (((1,), (1,)), ((), ())), precision=HIGHEST)

        def by_piece(value, axis):
            return jnp.stack([lax.dynamic_index_in_dim(value, t_at ^ j, axis, keepdims=False) for j in range(n_t)], axis=axis)

        vec = jnp.dot(vectors, turn32, precision=HIGHEST)
        vec_heads = by_piece(vectors.reshape(-1, n_t, cols), 1)
        bias_ff = by_piece(ffn_bias1.reshape(2, n_t, ff), 1)

        qv = jnp.zeros((3, n_t, 4 * cols), F32)
        for b in range(3):
            qv = qv.at[b, :, :cols].set(vec_heads[5 * b]).at[b, :, 2 * cols : 3 * cols].set(vec_heads[5 * b + 1])

        def rows3(row):
            return vec[row : row + 3]

        n_lang, n_visn = lang_in.shape[0], visn_in.shape[0]
        slots, regions = n_lang // items, n_visn // items
        item = jnp.concatenate([jnp.arange(n_lang) // slots, jnp.arange(n_visn) // regions])
        is_lang = jnp.arange(n_lang + n_visn) < n_lang
        seen = jnp.concatenate([usable.reshape(-1), jnp.ones((n_visn,), bool)])
        same = (item[:, None] == item[None, :]) & seen[None, :]
        mask0 = (same & (is_lang[:, None] != is_lang[None, :])).astype(F32)
        mask1 = same[:n_lang, :n_lang].astype(F32)
        mask2 = same[n_lang:, n_lang:].astype(F32)

        x0 = to_rel(jnp.concatenate([lang_in, visn_in], axis=0)).astype(F32)
        both1, *kept0 = att_forward(x0, mask0, qv[0], rows3(2), full["a0"], heads_here)
        lang1, visn1 = both1[:n_lang], both1[n_lang:]
        lang2, *kept1 = att_forward(lang1, mask1, qv[1], rows3(7), full["a1"], heads_here)
        visn2, *kept2 = att_forward(visn1, mask2, qv[2], rows3(12), full["a2"], heads_here)
        lang_out, gz_lang, sums15, act0, slope0 = ffn_forward(lang2, to_rel(lang_cot), bias_ff[0], rows3(15), full["u0"], full["d0"])
        visn_out, gz_visn, sums18, act1, slope1 = ffn_forward(visn2, to_rel(visn_cot), bias_ff[1], rows3(18), full["u1"], full["d1"])

        grads = {}
        inner1, bias_visn, dw = ffn_down_back(gz_visn, act1, slope1, full["d1"])
        grads["d1"] = tree.scatter(dw, orders["d1"])
        g_visn, dw = ffn_up_back(gz_visn, visn2, inner1, full["u1"])
        grads["u1"] = tree.scatter(dw, orders["u1"])
        inner0, bias_lang, dw = ffn_down_back(gz_lang, act0, slope0, full["d0"])
        grads["d0"] = tree.scatter(dw, orders["d0"])
        g_lang, dw = ffn_up_back(gz_lang, lang2, inner0, full["u0"])
        grads["u0"] = tree.scatter(dw, orders["u0"])
        g_visn, sums12, bias2, dw = att_backward(g_visn, visn1, mask2, rows3(12), kept2, full["a2"], heads_here)
        grads["a2"] = tree.scatter(dw, orders["a2"])
        g_lang, sums7, bias1, dw = att_backward(g_lang, lang1, mask1, rows3(7), kept1, full["a1"], heads_here)
        grads["a1"] = tree.scatter(dw, orders["a1"])
        g_both, sums2, bias0, dw = att_backward(jnp.concatenate([g_lang, g_visn], axis=0), x0, mask0, rows3(2), kept0, full["a0"], heads_here)
        grads["a0"] = tree.scatter(dw, orders["a0"])

        blank = jnp.zeros((2, width), F32)
        by_rows = to_abs(jnp.concatenate([blank, sums2[:3], blank, sums7[:3], blank, sums12[:3], sums15[:3], sums18[:3]], axis=0))
        hrows = {}
        for b, value in enumerate((bias0, bias1, bias2)):
            hrows[5 * b], hrows[5 * b + 1] = value[:, :cols], value[:, 2 * cols : 3 * cols]
        out_abs = to_abs(jnp.concatenate([lang_out, visn_out, g_both], axis=0))
        n_both = n_lang + n_visn
        lang_out, visn_out = out_abs[:n_lang], out_abs[n_lang:n_both]
        lang_grad, visn_grad = out_abs[n_both : n_both + n_lang], out_abs[n_both + n_lang :]

        for row, value in hrows.items():
            by_rows = by_rows.at[row].set(by_piece(value, 0).reshape(-1))
        bias_all = by_piece(jnp.stack([bias_lang, bias_visn]), 1)
        sums = tree.total(jnp.concatenate([by_rows, bias_all.reshape(-1, width)], axis=0))
        vector_grad, bias1_grad = sums[:21], sums[21:].reshape(ffn_bias1.shape)

        share_in = jnp.stack([grads["a%d" % b][:, : 3 * cols].astype(F32).reshape(rows, 3, cols) for b in range(3)])
        share_out = jnp.stack([grads["a%d" % b][:, 3 * cols :].astype(F32).T for b in range(3)])
        share_up = jnp.stack([grads["u%d" % i].astype(F32) for i in range(2)])
        share_down = jnp.stack([grads["d%d" % i].astype(F32).T for i in range(2)])
        result = [lang_out, visn_out, lang_grad, visn_grad]
        for share, weight, first, second, rate in (
            (share_in, att_in, att_in_m, att_in_v, rate_in),
            (share_out, att_out, att_out_m, att_out_v, rate_out),
            (share_up, ffn_up, ffn_up_m, ffn_up_v, rate_up),
            (share_down, ffn_down, ffn_down_m, ffn_down_v, rate_down),
        ):
            m_new, v_new, w_new = adam_step(weight, share, first, second, rate)
            result += [share, m_new, v_new, w_new, w_new.astype(BF16)]
        for share, weight, first, second, rate in (
            (vector_grad, vectors, vectors_m, vectors_v, rate_vector),
            (bias1_grad, ffn_bias1, bias1_m, bias1_v, rate_bias),
        ):
            m_new, v_new, w_new = adam_step(weight, share, first, second, rate)
            result += [share, m_new, v_new, w_new]
        return tuple(result)

    return local


def solution(mesh):
    rows = P(("dp", "tensor"), None)
    w_in, w_out, w_up, w_down = P(None, "dp", None, "tensor"), P(None, "tensor", "dp"), P(None, "dp", "tensor"), P(None, "tensor", "dp")
    return jax.shard_map(
        make_local(mesh),
        mesh=mesh,
        in_specs=(rows, rows, P(("dp", "tensor")), rows, rows, w_in, w_out, w_up, w_down, P(), P())
        + (w_in,) * 2 + (w_out,) * 2 + (w_up,) * 2 + (w_down,) * 2 + (P(),) * 4,
        out_specs=(rows,) * 4 + (w_in,) * 5 + (w_out,) * 5 + (w_up,) * 5 + (w_down,) * 5 + (P(),) * 8,
        check_vma=False,
    )
```

time: 1230 us -> 740 us (0.60)
  waiting for transfers between devices: 671 us -> 241 us
  starting transfers between devices: 2.08 us -> 209 us
  matrix products: 143 us -> 8.58 us
  local copies, waits for them, and re-layouts: 205 us -> 80.9 us
  Pallas kernels: 0 us -> 124 us
  blocking collectives: 103 us -> 0 us
  between operations: 18.6 us -> 3.09 us
    reduce_scatter x13 -> x0, waiting for transfers between devices: 247 us -> none  [the longest x1 61.4 us: local(): lax.psum_scatter(grad_up.astype(jnp.bfloat16), 'dp', scatter_dimension=1,...]
    ppermute x0 -> x118, waiting for transfers between devices: none -> 241 us  [swap(): return lax.ppermute(value, axis, perm)]
    ppermute x0 -> x118, starting transfers between devices: none -> 209 us  [swap(): return lax.ppermute(value, axis, perm)]
    all_gather x9 -> x0, waiting for transfers between devices: 161 us -> none  [the longest x1 50 us: local(): lax.all_gather(ffn_down.astype(jnp.bfloat16), 'dp', axis=2, tiled=True)]
    unnamed x29 -> x0, waiting for transfers between devices: 139 us -> none
    dot_general x60 -> x6, matrix products: 143 us -> 8.58 us  [the longest x2 4.05 us: to_abs(): lax.dot_general(value, turn32, (((1,), (1,)), ((), ())), precision=HIGHEST)]
    psum x1 -> x0, waiting for transfers between devices: 124 us -> none  [local(): lax.psum((jnp.stack(vector_rows), bias1_local), ('dp', 'tensor'))]
    pallas_call x0 -> x12, Pallas kernels: none -> 124 us  [call(): pl.pallas_call(kernel, out_shape=tuple(outs), in_specs=[vmem] * len(args)...]
  transfers between devices with their start and end apart: 26 -> 118, of which waited for: 22 -> 34; matrix products, arithmetic and copies ran while one was open for 25% -> 19% of each run, Pallas kernels for 0% -> 9%
where the time goes in v1:
time: 740 us; the launch traced here: 731 us
  waiting for transfers between devices  241 us (33%)
  starting transfers between devices  209 us (28%)
  Pallas kernels  124 us (17%)
  local copies, waits for them, and re-layouts  80.9 us (11%)
  other arithmetic  64.4 us (9%)
  matrix products  8.58 us (1%)
    ppermute x118, waiting for transfers between devices, swap(): return lax.ppermute(value, axis, perm)  241 us
    ppermute x118, starting transfers between devices, swap(): return lax.ppermute(value, axis, perm)  209 us
    pallas_call x12, Pallas kernels, call(): pl.pallas_call(kernel, out_shape=tuple(outs), in_specs=[vmem] * len(args)...  124 us
    unnamed x290, local copies, waits for them, and re-layouts  36.6 us
    concatenate x15, other arithmetic, gather(): jnp.concatenate([v] + [self.swap(v, name, m) for m in range(1, size)], ax...  25.5 us
    convert_element_type x26, other arithmetic, scatter(): new[j] = total.astype(BF16)  17 us
  transfers between devices with their start and end apart: 118, of which 34 were waited for; matrix products, arithmetic and copies ran while one was open for 19% of the time, Pallas kernels for 9%

profile of v1, /device:TPU:0, one launch (start us, length us, event | category | flops | bytes accessed | tf_op | source)
XLA Modules:
  0.0 731.1 jit_solution(3899947970135728149)
XLA Ops:
  24.9 12.3 %collective-permute-start.37 = (bf16[1,1,96,768]{3,2,1,0:T(8,128)(2,1)S(1)}, bf16[1,1,96,768]{3,2,1,0:T(8,128)(2,1)S(1)}, u32[]{:S(2)}, u32[]{:S(2)}) collective-permute-start(bf16[1,1,96,768]{3,2,1,0:T(8,128)(2,1)S(1)} %get-tuple-element.467), channel_id=1, source_target_pairs={{0,8},{4,12},{8,0},{12,4},{16,24},{20,28},{24,16},{28,20},{1,9},{5... | collective-permute-start | bytes 442376 | tf_op jit(solution)/shard_map/ppermute | solution.py:52
  45.8 6.9 collective-permute-start.7
  68.6 7.5 %collective-permute-done.8 = bf16[1,1,96,768]{2,3,1,0:T(8,128)(2,1)S(1)} collective-permute-done((bf16[1,1,96,768]{2,3,1,0:T(8,128)(2,1)S(1)}, bf16[1,1,96,768]{2,3,1,0:T(8,128)(2,1)S(1)}, u32[]{:S(2)}, u32[]{:S(2)}) %collective-permute-start.8) | collective-permute-done | bytes 147488 | tf_op jit(solution)/shard_map/ppermute | solution.py:52
  101.9 8.4 %collective-permute-start.52 = (bf16[2,1,96,768]{3,2,1,0:T(8,128)(2,1)}, bf16[2,1,96,768]{3,2,1,0:T(8,128)(2,1)}, u32[]{:S(2)}, u32[]{:S(2)}) collective-permute-start(bf16[2,1,96,768]{3,2,1,0:T(8,128)(2,1)} %constant_dynamic-update-slice_fusion.6), channel_id=1, source_target_pairs={{0,8},{4,12},{8,0},{12,4},{16,24},{20,28},{24,16},{28,20},{1,9},{5... | collective-permute-start | bytes 884744 | tf_op jit(solution)/shard_map/ppermute | solution.py:52
  162.2 6.3 collective-permute-done.20
  169.1 12.6 %collective-permute-done.26 = bf16[1,4,96,768]{3,2,1,0:T(8,128)(2,1)} collective-permute-done((bf16[1,4,96,768]{3,2,1,0:T(8,128)(2,1)}, bf16[1,4,96,768]{3,2,1,0:T(8,128)(2,1)}, u32[]{:S(2)}, u32[]{:S(2)}) %collective-permute-start.26) | collective-permute-done | bytes 589856 | tf_op jit(solution)/shard_map/ppermute | solution.py:52
  185.8 8.5 %collective-permute-done.43 = bf16[1,4,96,768]{3,2,1,0:T(8,128)(2,1)S(1)} collective-permute-done((bf16[1,4,96,768]{3,2,1,0:T(8,128)(2,1)}, bf16[1,4,96,768]{3,2,1,0:T(8,128)(2,1)S(1)}, u32[]{:S(2)}, u32[]{:S(2)}) %collective-permute-start.43) | collective-permute-done | bytes 589856 | tf_op jit(solution)/shard_map/ppermute | solution.py:52
  194.2 12.6 %collective-permute-done.13 = bf16[1,4,96,768]{3,2,1,0:T(8,128)(2,1)S(1)} collective-permute-done((bf16[1,4,96,768]{3,2,1,0:T(8,128)(2,1)}, bf16[1,4,96,768]{3,2,1,0:T(8,128)(2,1)S(1)}, u32[]{:S(2)}, u32[]{:S(2)}) %collective-permute-start.13) | collective-permute-done | bytes 589856 | tf_op jit(solution)/shard_map/ppermute | solution.py:52
  206.9 9.2 %collective-permute-done.21 = bf16[1,4,96,768]{3,2,1,0:T(8,128)(2,1)S(1)} collective-permute-done((bf16[1,4,96,768]{3,2,1,0:T(8,128)(2,1)}, bf16[1,4,96,768]{3,2,1,0:T(8,128)(2,1)S(1)}, u32[]{:S(2)}, u32[]{:S(2)}) %collective-permute-start.21) | collective-permute-done | bytes 589856 | tf_op jit(solution)/shard_map/ppermute | solution.py:52
  246.5 12.6 %shard_map.479 = (f32[336,768]{1,0:T(8,128)}, f32[336,768]{1,0:T(8,128)}, f32[336,128]{1,0:T(8,128)S(1)}, bf16[4,336,768]{2,1,0:T(8,128)(2,1)}, bf16[4,336,256]{2,1,0:T(8,128)(2,1)S(1)}) custom-call(f32[336,768]{1,0:T(8,128)} %fusion.26.x_ref, f32[336,336]{1,0:T(8,128)S(1)} %get-tuple-element.528.mask_ref, f32[4,768]{1,0:T(4,128)S(1)} %get-tuple-element.486.bias_ref, ...), custom_call_target="tpu_custom_call" | custom-call | flops 1585446912 | bytes 11212800 | tf_op jit(solution)/shard_map/pallas_call | solution.py:252
  261.4 9.7 %shard_map.482 = (f32[216,768]{1,0:T(8,128)S(1)}, f32[216,768]{1,0:T(8,128)}, f32[216,128]{1,0:T(8,128)S(1)}, bf16[4,216,768]{2,1,0:T(8,128)(2,1)}, bf16[4,216,256]{2,1,0:T(8,128)(2,1)S(1)}) custom-call(f32[216,768]{1,0:T(8,128)} %slice.601.x_ref, f32[216,216]{1,0:T(8,128)S(1)} %slice_convert_fusion.mask_ref, f32[4,768]{1,0:T(4,128)S(1)} %get-tuple-element.485.bias_ref, ...), custom_call_target="tpu_custom_call" | custom-call | flops 1019215872 | bytes 8797440 | tf_op jit(solution)/shard_map/pallas_call | solution.py:252
  272.8 8.5 %shard_map.483 = (f32[216,768]{1,0:T(8,128)S(1)}, f32[216,768]{1,0:T(8,128)S(1)}, f32[8,768]{1,0:T(8,128)S(1)}, bf16[4,216,768]{2,1,0:T(8,128)(2,1)}, f32[4,216,768]{2,1,0:T(8,128)}) custom-call(f32[216,768]{1,0:T(8,128)} %copy-done.4, bf16[216,768]{1,0:T(8,128)(2,1)S(1)} %fusion.28.cot_ref, f32[4,768]{1,0:T(4,128)S(1)} %get-tuple-element.492.bias_ref, ...), custom_call_target="tpu_custom_call" | custom-call | flops 2038431744 | bytes 15787008 | tf_op jit(solution)/shard_map/pallas_call | solution.py:252
  283.6 7.3 %shard_map.487 = (bf16[4,216,768]{2,1,0:T(8,128)(2,1)}, f32[4,768]{1,0:T(4,128)S(1)}, bf16[768,768]{1,0:T(8,128)(2,1)S(1)}, bf16[768,768]{1,0:T(8,128)(2,1)}, bf...) custom-call(f32[216,768]{1,0:T(8,128)S(1)} %get-tuple-element.259.gz_ref, ...), custom_call_target="tpu_custom_call" | custom-call | flops 2038431744 | bytes 15421440 | tf_op jit(solution)/shard_map/pallas_call | solution.py:252
  290.9 6.3 shard_map.488
  298.1 16.1 %shard_map.489 = (f32[216,768]{1,0:T(8,128)S(1)}, f32[8,768]{1,0:T(8,128)S(1)}, f32[4,768]{1,0:T(4,128)S(1)}, bf16[768,768]{1,0:T(8,128)(2,1)}, bf16[768,768]{1,...) custom-call(f32[216,768]{1,0:T(8,128)} %copy-done.3, f32[216,768]{1,0:T(8,128)} %slice.601.x_ref, ...), custom_call_target="tpu_custom_call" | custom-call | flops 2038431744 | bytes 14204160 | tf_op jit(solution)/shard_map/pallas_call | solution.py:252
  314.4 8.1 %shard_map.480 = (f32[120,768]{1,0:T(8,128)S(1)}, f32[120,768]{1,0:T(8,128)S(1)}, f32[120,128]{1,0:T(8,128)S(1)}, bf16[4,120,768]{2,1,0:T(8,128)(2,1)}, bf16[4,120,256]{2,1,0:T(8,128)(2,1)S(1)}) custom-call(f32[120,768]{1,0:T(8,128)S(1)} %slice.591.x_ref, f32[120,120]{1,0:T(8,128)S(1)} %slice_convert_fusion.1.mask_ref, ...), custom_call_target="tpu_custom_call" | custom-call | flops 566231040 | bytes 6948096 | tf_op jit(solution)/shard_map/pallas_call | solution.py:252
  322.6 7.4 %shard_map.481 = (f32[120,768]{1,0:T(8,128)S(1)}, f32[120,768]{1,0:T(8,128)S(1)}, f32[8,768]{1,0:T(8,128)S(1)}, bf16[4,120,768]{2,1,0:T(8,128)(2,1)}, f32[4,120,768]{2,1,0:T(8,128)}) custom-call(f32[120,768]{1,0:T(8,128)S(1)} %get-tuple-element.245.x_ref, bf16[120,768]{1,0:T(8,128)(2,1)S(1)} %fusion.36.cot_ref, f32[4,768]{1,0:T(4,128)S(1)} %get-tuple-element.491.bias_ref, ...), custom_call_target="tpu_custom_call" | custom-call | flops 1132462080 | bytes 12985344 | tf_op jit(solution)/shard_map/pallas_call | solution.py:252
  331.3 6.2 shard_map.484
  337.5 6.0 shard_map.485
  343.4 12.3 %shard_map.486 = (f32[120,768]{1,0:T(8,128)S(1)}, f32[8,768]{1,0:T(8,128)S(1)}, f32[4,768]{1,0:T(4,128)S(1)}, bf16[768,768]{1,0:T(8,128)(2,1)}, bf16[768,768]{1,...) custom-call(f32[120,768]{1,0:T(8,128)S(1)} %get-tuple-element.253.g_ref, ...), custom_call_target="tpu_custom_call" | custom-call | flops 1132462080 | bytes 12059904 | tf_op jit(solution)/shard_map/pallas_call | solution.py:252
  358.1 23.0 %shard_map.490 = (f32[336,768]{1,0:T(8,128)}, f32[8,768]{1,0:T(8,128)S(1)}, f32[4,768]{1,0:T(4,128)S(1)}, bf16[768,768]{1,0:T(8,128)(2,1)}, bf16[768,768]{1,0:T(...) custom-call(f32[336,768]{1,0:T(8,128)} %pad_maximum_fusion.8.g_ref, f32[336,768]{1,0:T(8,128)} %fusion.26.x_ref, ...), custom_call_target="tpu_custom_call" | custom-call | flops 3170893824 | bytes 16988160 | tf_op jit(solution)/shard_map/pallas_call | solution.py:252
  451.6 9.0 %collective-permute-done.103 = bf16[2,1,96,768]{3,2,1,0:T(8,128)(2,1)S(1)} collective-permute-done((bf16[2,1,96,768]{3,2,1,0:T(8,128)(2,1)S(1)}, bf16[2,1,96,768]{3,2,1,0:T(8,128)(2,1)S(1)}, u32[]{:S(2)}, u32[]{:S(2)}) %collective-permute-start.103) | collective-permute-done | bytes 294944 | tf_op jit(solution)/shard_map/ppermute | solution.py:52
  464.4 21.4 %collective-permute-done.108 = bf16[2,1,96,768]{3,2,1,0:T(8,128)(2,1)S(1)} collective-permute-done((bf16[2,1,96,768]{3,2,1,0:T(8,128)(2,1)S(1)}, bf16[2,1,96,768]{3,2,1,0:T(8,128)(2,1)S(1)}, u32[]{:S(2)}, u32[]{:S(2)}) %collective-permute-start.108) | collective-permute-done | bytes 294944 | tf_op jit(solution)/shard_map/ppermute | solution.py:52
  489.2 22.8 %collective-permute-done.110 = bf16[1,1,96,768]{3,2,1,0:T(8,128)(2,1)S(1)} collective-permute-done((bf16[1,1,96,768]{3,2,1,0:T(8,128)(2,1)S(1)}, bf16[1,1,96,768]{3,2,1,0:T(8,128)(2,1)S(1)}, u32[]{:S(2)}, u32[]{:S(2)}) %collective-permute-start.110) | collective-permute-done | bytes 147488 | tf_op jit(solution)/shard_map/ppermute | solution.py:52
  514.4 13.2 %collective-permute-done.111 = bf16[1,1,96,768]{3,2,1,0:T(8,128)(2,1)S(1)} collective-permute-done((bf16[1,1,96,768]{3,2,1,0:T(8,128)(2,1)S(1)}, bf16[1,1,96,768]{3,2,1,0:T(8,128)(2,1)S(1)}, u32[]{:S(2)}, u32[]{:S(2)}) %collective-permute-start.111) | collective-permute-done | bytes 147488 | tf_op jit(solution)/shard_map/ppermute | solution.py:52
  545.5 11.7 %collective-permute-done.67 = bf16[1,4,96,768]{3,2,1,0:T(8,128)(2,1)S(1)} collective-permute-done((bf16[1,4,96,768]{3,2,1,0:T(8,128)(2,1)S(1)}, bf16[1,4,96,768]{3,2,1,0:T(8,128)(2,1)S(1)}, u32[]{:S(2)}, u32[]{:S(2)}) %collective-permute-start.67) | collective-permute-done | bytes 589856 | tf_op jit(solution)/shard_map/ppermute | solution.py:52
  559.6 22.8 %collective-permute-done.96 = bf16[2,4,96,768]{3,2,1,0:T(8,128)(2,1)S(1)} collective-permute-done((bf16[2,4,96,768]{3,2,1,0:T(8,128)(2,1)S(1)}, bf16[2,4,96,768]{3,2,1,0:T(8,128)(2,1)S(1)}, u32[]{:S(2)}, u32[]{:S(2)}) %collective-permute-start.96) | collective-permute-done | bytes 1179680 | tf_op jit(solution)/shard_map/ppermute | solution.py:52
  582.5 12.6 %collective-permute-start.83 = (bf16[1,1,96,768]{3,2,1,0:T(8,128)(2,1)S(1)}, bf16[1,1,96,768]{3,2,1,0:T(8,128)(2,1)S(1)}, u32[]{:S(2)}, u32[]{:S(2)}) collective-permute-start(bf16[1,1,96,768]{3,2,1,0:T(8,128)(2,1)S(1)} %get-tuple-element.446), channel_id=1, source_target_pairs={{0,8},{4,12},{8,0},{12,4},{16,24},{20,28},{24,16},{28,20},{1,9},{5... | collective-permute-start | bytes 442376 | tf_op jit(solution)/shard_map/ppermute | solution.py:52
  597.8 10.0 %collective-permute-done.58 = bf16[2,4,96,768]{3,2,1,0:T(8,128)(2,1)S(1)} collective-permute-done((bf16[2,4,96,768]{3,2,1,0:T(8,128)(2,1)S(1)}, bf16[2,4,96,768]{3,2,1,0:T(8,128)(2,1)S(1)}, u32[]{:S(2)}, u32[]{:S(2)}) %collective-permute-start.58) | collective-permute-done | bytes 1179680 | tf_op jit(solution)/shard_map/ppermute | solution.py:52
  607.7 9.3 %collective-permute-start.85 = (bf16[1,1,96,768]{3,2,1,0:T(8,128)(2,1)S(1)}, bf16[1,1,96,768]{3,2,1,0:T(8,128)(2,1)S(1)}, u32[]{:S(2)}, u32[]{:S(2)}) collective-permute-start(bf16[1,1,96,768]{3,2,1,0:T(8,128)(2,1)S(1)} %get-tuple-element.447), channel_id=1, source_target_pairs={{0,24},{4,28},{8,16},{12,20},{16,8},{20,12},{24,0},{28,4},{1,25},{... | collective-permute-start | bytes 442376 | tf_op jit(solution)/shard_map/ppermute | solution.py:52
  617.5 6.1 collective-permute-start.91
  625.4 18.1 %collective-permute-start.92 = (bf16[1,1,96,768]{3,2,1,0:T(8,128)(2,1)S(1)}, bf16[1,1,96,768]{3,2,1,0:T(8,128)(2,1)S(1)}, u32[]{:S(2)}, u32[]{:S(2)}) collective-permute-start(bf16[1,1,96,768]{3,2,1,0:T(8,128)(2,1)S(1)} %get-tuple-element.451), channel_id=1, source_target_pairs={{0,16},{4,20},{8,24},{12,28},{16,0},{20,4},{24,8},{28,12},{1,17},{... | collective-permute-start | bytes 442376 | tf_op jit(solution)/shard_map/ppermute | solution.py:52
  (701 shorter events, 363.1 us)
Async XLA Ops:
  100.5 36.8 %collective-permute-start.3 = (bf16[1,4,96,768]{3,2,1,0:T(8,128)(2,1)}, bf16[1,4,96,768]{3,2,1,0:T(8,128)(2,1)}, u32[]{:S(2)}, u32[]{:S(2)}) collective-permute-start(bf16[1,4,96,768]{3,2,1,0:T(8,128)(2,1)} %copy.177), channel_id=1, source_target_pairs={{0,4},{4,0},{8,12},{12,8},{16,20},{20,16},{24,28},{28,24},{1,5},{5... | collective-permute-start | bytes 1769480 | tf_op jit(solution)/shard_map/ppermute | solution.py:52
  157.9 58.2 %collective-permute-start.5 = (bf16[2,4,96,768]{3,2,1,0:T(8,128)(2,1)}, bf16[2,4,96,768]{3,2,1,0:T(8,128)(2,1)}, u32[]{:S(2)}, u32[]{:S(2)}) collective-permute-start(bf16[2,4,96,768]{3,2,1,0:T(8,128)(2,1)} %copy.179), channel_id=1, source_target_pairs={{0,2},{1,3},{2,0},{3,1},{4,6},{5,7},{6,4},{7,5},{8,10},{9,11},{10,... | collective-permute-start | bytes 3538952 | tf_op jit(solution)/shard_map/ppermute | solution.py:52
  159.4 57.3 %collective-permute-start.35 = (bf16[2,4,96,768]{3,2,1,0:T(8,128)(2,1)}, bf16[2,4,96,768]{3,2,1,0:T(8,128)(2,1)}, u32[]{:S(2)}, u32[]{:S(2)}) collective-permute-start(bf16[2,4,96,768]{3,2,1,0:T(8,128)(2,1)} %copy.191), channel_id=1, source_target_pairs={{0,2},{1,3},{2,0},{3,1},{4,6},{5,7},{6,4},{7,5},{8,10},{9,11},{10,... | collective-permute-start | bytes 3538952 | tf_op jit(solution)/shard_map/ppermute | solution.py:52
  182.2 33.8 %collective-permute-start.21 = (bf16[1,4,96,768]{3,2,1,0:T(8,128)(2,1)}, bf16[1,4,96,768]{3,2,1,0:T(8,128)(2,1)S(1)}, u32[]{:S(2)}, u32[]{:S(2)}) collective-permute-start(bf16[1,4,96,768]{3,2,1,0:T(8,128)(2,1)} %collective-permute-done.20), channel_id=1, source_target_pairs={{0,4},{4,0},{8,12},{12,8},{16,20},{20,16},{24,28},{28,24},{1,5},{5... | collective-permute-start | bytes 1769480 | tf_op jit(solution)/shard_map/ppermute | solution.py:52
  194.2 36.0 %collective-permute-start.49 = (bf16[2,4,96,768]{3,2,1,0:T(8,128)(2,1)S(1)}, bf16[2,4,96,768]{3,2,1,0:T(8,128)(2,1)}, u32[]{:S(2)}, u32[]{:S(2)}) collective-permute-start(bf16[2,4,96,768]{3,2,1,0:T(8,128)(2,1)S(1)} %pad_maximum_fusion.6), channel_id=1, source_target_pairs={{0,1},{1,0},{2,3},{3,2},{4,5},{5,4},{6,7},{7,6},{8,9},{9,8},{10,11... | collective-permute-start | bytes 3538952 | tf_op jit(solution)/shard_map/ppermute | solution.py:52
  230.2 41.8 %collective-permute-start.55 = (bf16[2,4,96,768]{3,2,1,0:T(8,128)(2,1)}, bf16[2,4,96,768]{3,2,1,0:T(8,128)(2,1)}, u32[]{:S(2)}, u32[]{:S(2)}) collective-permute-start(bf16[2,4,96,768]{3,2,1,0:T(8,128)(2,1)} %pad_maximum_fusion.7), channel_id=1, source_target_pairs={{0,1},{1,0},{2,3},{3,2},{4,5},{5,4},{6,7},{7,6},{8,9},{9,8},{10,11... | collective-permute-start | bytes 3538952 | tf_op jit(solution)/shard_map/ppermute | solution.py:52
  230.6 41.5 %collective-permute-start.41 = (bf16[2,4,96,768]{3,2,1,0:T(8,128)(2,1)}, bf16[2,4,96,768]{3,2,1,0:T(8,128)(2,1)}, u32[]{:S(2)}, u32[]{:S(2)}) collective-permute-start(bf16[2,4,96,768]{3,2,1,0:T(8,128)(2,1)} %pad_maximum_fusion.5), channel_id=1, source_target_pairs={{0,1},{1,0},{2,3},{3,2},{4,5},{5,4},{6,7},{7,6},{8,9},{9,8},{10,11... | collective-permute-start | bytes 3538952 | tf_op jit(solution)/shard_map/ppermute | solution.py:52
  230.7 41.9 %collective-permute-start.44 = (bf16[2,4,96,768]{3,2,1,0:T(8,128)(2,1)}, bf16[2,4,96,768]{3,2,1,0:T(8,128)(2,1)}, u32[]{:S(2)}, u32[]{:S(2)}) collective-permute-start(bf16[2,4,96,768]{3,2,1,0:T(8,128)(2,1)} %constant_dynamic-update-slice_fusion.4), channel_id=1, source_target_pairs={{0,1},{1,0},{2,3},{3,2},{4,5},{5,4},{6,7},{7,6},{8,9},{9,8},{10,11... | collective-permute-start | bytes 3538952 | tf_op jit(solution)/shard_map/ppermute | solution.py:52
  236.5 46.1 %collective-permute-start.11 = (bf16[2,4,96,768]{3,2,1,0:T(8,128)(2,1)}, bf16[2,4,96,768]{3,2,1,0:T(8,128)(2,1)S(1)}, u32[]{:S(2)}, u32[]{:S(2)}) collective-permute-start(bf16[2,4,96,768]{3,2,1,0:T(8,128)(2,1)} %copy.185), channel_id=1, source_target_pairs={{0,1},{1,0},{2,3},{3,2},{4,5},{5,4},{6,7},{7,6},{8,9},{9,8},{10,11... | collective-permute-start | bytes 3538952 | tf_op jit(solution)/shard_map/ppermute | solution.py:52
  236.6 46.4 %collective-permute-start.28 = (bf16[2,4,96,768]{3,2,1,0:T(8,128)(2,1)}, bf16[2,4,96,768]{3,2,1,0:T(8,128)(2,1)}, u32[]{:S(2)}, u32[]{:S(2)}) collective-permute-start(bf16[2,4,96,768]{3,2,1,0:T(8,128)(2,1)} %pad_maximum_fusion.4), channel_id=1, source_target_pairs={{0,2},{1,3},{2,0},{3,1},{4,6},{5,7},{6,4},{7,5},{8,10},{9,11},{10,... | collective-permute-start | bytes 3538952 | tf_op jit(solution)/shard_map/ppermute | solution.py:52
  272.0 50.6 %collective-permute-start.27 = (bf16[2,4,96,768]{3,2,1,0:T(8,128)(2,1)}, bf16[2,4,96,768]{3,2,1,0:T(8,128)(2,1)}, u32[]{:S(2)}, u32[]{:S(2)}) collective-permute-start(bf16[2,4,96,768]{3,2,1,0:T(8,128)(2,1)} %pad_maximum_fusion.4), channel_id=1, source_target_pairs={{0,1},{1,0},{2,3},{3,2},{4,5},{5,4},{6,7},{7,6},{8,9},{9,8},{10,11... | collective-permute-start | bytes 3538952 | tf_op jit(solution)/shard_map/ppermute | solution.py:52
  272.1 50.4 %collective-permute-start.19 = (bf16[2,4,96,768]{3,2,1,0:T(8,128)(2,1)}, bf16[2,4,96,768]{3,2,1,0:T(8,128)(2,1)}, u32[]{:S(2)}, u32[]{:S(2)}) collective-permute-start(bf16[2,4,96,768]{3,2,1,0:T(8,128)(2,1)} %pad_maximum_fusion.3), channel_id=1, source_target_pairs={{0,1},{1,0},{2,3},{3,2},{4,5},{5,4},{6,7},{7,6},{8,9},{9,8},{10,11... | collective-permute-start | bytes 3538952 | tf_op jit(solution)/shard_map/ppermute | solution.py:52
  272.7 41.8 %collective-permute-start.14 = (bf16[2,4,96,768]{3,2,1,0:T(8,128)(2,1)}, bf16[2,4,96,768]{3,2,1,0:T(8,128)(2,1)}, u32[]{:S(2)}, u32[]{:S(2)}) collective-permute-start(bf16[2,4,96,768]{3,2,1,0:T(8,128)(2,1)} %constant_dynamic-update-slice_fusion), channel_id=1, source_target_pairs={{0,1},{1,0},{2,3},{3,2},{4,5},{5,4},{6,7},{7,6},{8,9},{9,8},{10,11... | collective-permute-start | bytes 3538952 | tf_op jit(solution)/shard_map/ppermute | solution.py:52
  282.6 40.0 %collective-permute-start.22 = (bf16[2,4,96,768]{3,2,1,0:T(8,128)(2,1)}, bf16[2,4,96,768]{3,2,1,0:T(8,128)(2,1)}, u32[]{:S(2)}, u32[]{:S(2)}) collective-permute-start(bf16[2,4,96,768]{3,2,1,0:T(8,128)(2,1)} %constant_dynamic-update-slice_fusion.2), channel_id=1, source_target_pairs={{0,1},{1,0},{2,3},{3,2},{4,5},{5,4},{6,7},{7,6},{8,9},{9,8},{10,11... | collective-permute-start | bytes 3538952 | tf_op jit(solution)/shard_map/ppermute | solution.py:52
  283.0 39.6 %collective-permute-start.29 = (bf16[2,4,96,768]{3,2,1,0:T(8,128)(2,1)}, bf16[2,4,96,768]{3,2,1,0:T(8,128)(2,1)}, u32[]{:S(2)}, u32[]{:S(2)}) collective-permute-start(bf16[2,4,96,768]{3,2,1,0:T(8,128)(2,1)} %collective-permute-done.28), channel_id=1, source_target_pairs={{0,1},{1,0},{2,3},{3,2},{4,5},{5,4},{6,7},{7,6},{8,9},{9,8},{10,11... | collective-permute-start | bytes 3538952 | tf_op jit(solution)/shard_map/ppermute | solution.py:52
  442.9 42.9 %collective-permute-start.108 = (bf16[2,1,96,768]{3,2,1,0:T(8,128)(2,1)S(1)}, bf16[2,1,96,768]{3,2,1,0:T(8,128)(2,1)S(1)}, u32[]{:S(2)}, u32[]{:S(2)}) collective-permute-start(bf16[2,1,96,768]{3,2,1,0:T(8,128)(2,1)S(1)} %get-tuple-element.442), channel_id=1, source_target_pairs={{0,16},{4,20},{8,24},{12,28},{16,0},{20,4},{24,8},{28,12},{1,17},{... | collective-permute-start | bytes 884744 | tf_op jit(solution)/shard_map/ppermute | solution.py:52
  450.2 36.6 %collective-permute-start.109 = (bf16[2,1,96,768]{3,2,1,0:T(8,128)(2,1)S(1)}, bf16[2,1,96,768]{3,2,1,0:T(8,128)(2,1)S(1)}, u32[]{:S(2)}, u32[]{:S(2)}) collective-permute-start(bf16[2,1,96,768]{3,2,1,0:T(8,128)(2,1)S(1)} %get-tuple-element.441), channel_id=1, source_target_pairs={{0,24},{4,28},{8,16},{12,20},{16,8},{20,12},{24,0},{28,4},{1,25},{... | collective-permute-start | bytes 884744 | tf_op jit(solution)/shard_map/ppermute | solution.py:52
  462.1 67.3 %collective-permute-start.79 = (bf16[1,4,96,768]{3,2,1,0:T(8,128)(2,1)S(1)}, bf16[1,4,96,768]{3,2,1,0:T(8,128)(2,1)S(1)}, u32[]{:S(2)}, u32[]{:S(2)}) collective-permute-start(bf16[1,4,96,768]{3,2,1,0:T(8,128)(2,1)S(1)} %slice.741), channel_id=1, source_target_pairs={{0,4},{4,0},{8,12},{12,8},{16,20},{20,16},{24,28},{28,24},{1,5},{5... | collective-permute-start | bytes 1769480 | tf_op jit(solution)/shard_map/ppermute | solution.py:52
  463.4 49.3 %collective-permute-start.89 = (bf16[1,4,96,768]{3,2,1,0:T(8,128)(2,1)S(1)}, bf16[1,4,96,768]{3,2,1,0:T(8,128)(2,1)S(1)}, u32[]{:S(2)}, u32[]{:S(2)}) collective-permute-start(bf16[1,4,96,768]{3,2,1,0:T(8,128)(2,1)S(1)} %slice.751), channel_id=1, source_target_pairs={{0,4},{4,0},{8,12},{12,8},{16,20},{20,16},{24,28},{28,24},{1,5},{5... | collective-permute-start | bytes 1769480 | tf_op jit(solution)/shard_map/ppermute | solution.py:52
  485.8 43.1 %collective-permute-start.66 = (bf16[1,4,96,768]{3,2,1,0:T(8,128)(2,1)S(1)}, bf16[1,4,96,768]{3,2,1,0:T(8,128)(2,1)S(1)}, u32[]{:S(2)}, u32[]{:S(2)}) collective-permute-start(bf16[1,4,96,768]{3,2,1,0:T(8,128)(2,1)S(1)} %slice.724), channel_id=1, source_target_pairs={{0,4},{4,0},{8,12},{12,8},{16,20},{20,16},{24,28},{28,24},{1,5},{5... | collective-permute-start | bytes 1769480 | tf_op jit(solution)/shard_map/ppermute | solution.py:52
  514.3 43.7 %collective-permute-start.94 = (bf16[2,4,96,768]{3,2,1,0:T(8,128)(2,1)S(1)}, bf16[2,4,96,768]{3,2,1,0:T(8,128)(2,1)S(1)}, u32[]{:S(2)}, u32[]{:S(2)}) collective-permute-start(bf16[2,4,96,768]{3,2,1,0:T(8,128)(2,1)S(1)} %bitcast.198), channel_id=1, source_target_pairs={{0,1},{1,0},{2,3},{3,2},{4,5},{5,4},{6,7},{7,6},{8,9},{9,8},{10,11... | collective-permute-start | bytes 3538952 | tf_op jit(solution)/shard_map/ppermute | solution.py:52
  538.8 56.8 %collective-permute-start.56 = (bf16[2,4,96,768]{3,2,1,0:T(8,128)(2,1)S(1)}, bf16[2,4,96,768]{3,2,1,0:T(8,128)(2,1)S(1)}, u32[]{:S(2)}, u32[]{:S(2)}) collective-permute-start(bf16[2,4,96,768]{3,2,1,0:T(8,128)(2,1)S(1)} %bitcast.199), channel_id=1, source_target_pairs={{0,1},{1,0},{2,3},{3,2},{4,5},{5,4},{6,7},{7,6},{8,9},{9,8},{10,11... | collective-permute-start | bytes 3538952 | tf_op jit(solution)/shard_map/ppermute | solution.py:52
  544.5 37.9 %collective-permute-start.96 = (bf16[2,4,96,768]{3,2,1,0:T(8,128)(2,1)S(1)}, bf16[2,4,96,768]{3,2,1,0:T(8,128)(2,1)S(1)}, u32[]{:S(2)}, u32[]{:S(2)}) collective-permute-start(bf16[2,4,96,768]{3,2,1,0:T(8,128)(2,1)S(1)} %fusion.2), channel_id=1, source_target_pairs={{0,2},{1,3},{2,0},{3,1},{4,6},{5,7},{6,4},{7,5},{8,10},{9,11},{10,... | collective-permute-start | bytes 3538952 | tf_op jit(solution)/shard_map/ppermute | solution.py:52
  545.4 72.2 %collective-permute-start.71 = (bf16[2,4,96,768]{3,2,1,0:T(8,128)(2,1)S(1)}, bf16[2,4,96,768]{3,2,1,0:T(8,128)(2,1)S(1)}, u32[]{:S(2)}, u32[]{:S(2)}) collective-permute-start(bf16[2,4,96,768]{3,2,1,0:T(8,128)(2,1)S(1)} %bitcast.197), channel_id=1, source_target_pairs={{0,1},{1,0},{2,3},{3,2},{4,5},{5,4},{6,7},{7,6},{8,9},{9,8},{10,11... | collective-permute-start | bytes 3538952 | tf_op jit(solution)/shard_map/ppermute | solution.py:52
  557.2 50.6 %collective-permute-start.58 = (bf16[2,4,96,768]{3,2,1,0:T(8,128)(2,1)S(1)}, bf16[2,4,96,768]{3,2,1,0:T(8,128)(2,1)S(1)}, u32[]{:S(2)}, u32[]{:S(2)}) collective-permute-start(bf16[2,4,96,768]{3,2,1,0:T(8,128)(2,1)S(1)} %fusion.12), channel_id=1, source_target_pairs={{0,2},{1,3},{2,0},{3,1},{4,6},{5,7},{6,4},{7,5},{8,10},{9,11},{10,... | collective-permute-start | bytes 3538952 | tf_op jit(solution)/shard_map/ppermute | solution.py:52
  558.0 67.4 %collective-permute-start.73 = (bf16[2,4,96,768]{3,2,1,0:T(8,128)(2,1)S(1)}, bf16[2,4,96,768]{3,2,1,0:T(8,128)(2,1)S(1)}, u32[]{:S(2)}, u32[]{:S(2)}) collective-permute-start(bf16[2,4,96,768]{3,2,1,0:T(8,128)(2,1)S(1)} %fusion.8), channel_id=1, source_target_pairs={{0,2},{1,3},{2,0},{3,1},{4,6},{5,7},{6,4},{7,5},{8,10},{9,11},{10,... | collective-permute-start | bytes 3538952 | tf_op jit(solution)/shard_map/ppermute | solution.py:52
  582.5 64.1 %collective-permute-start.83 = (bf16[1,1,96,768]{3,2,1,0:T(8,128)(2,1)S(1)}, bf16[1,1,96,768]{3,2,1,0:T(8,128)(2,1)S(1)}, u32[]{:S(2)}, u32[]{:S(2)}) collective-permute-start(bf16[1,1,96,768]{3,2,1,0:T(8,128)(2,1)S(1)} %get-tuple-element.446), channel_id=1, source_target_pairs={{0,8},{4,12},{8,0},{12,4},{16,24},{20,28},{24,16},{28,20},{1,9},{5... | collective-permute-start | bytes 442376 | tf_op jit(solution)/shard_map/ppermute | solution.py:52
  595.6 51.1 %collective-permute-start.84 = (bf16[1,1,96,768]{3,2,1,0:T(8,128)(2,1)S(1)}, bf16[1,1,96,768]{3,2,1,0:T(8,128)(2,1)S(1)}, u32[]{:S(2)}, u32[]{:S(2)}) collective-permute-start(bf16[1,1,96,768]{3,2,1,0:T(8,128)(2,1)S(1)} %get-tuple-element.448), channel_id=1, source_target_pairs={{0,16},{4,20},{8,24},{12,28},{16,0},{20,4},{24,8},{28,12},{1,17},{... | collective-permute-start | bytes 442376 | tf_op jit(solution)/shard_map/ppermute | solution.py:52
  607.7 39.5 %collective-permute-start.85 = (bf16[1,1,96,768]{3,2,1,0:T(8,128)(2,1)S(1)}, bf16[1,1,96,768]{3,2,1,0:T(8,128)(2,1)S(1)}, u32[]{:S(2)}, u32[]{:S(2)}) collective-permute-start(bf16[1,1,96,768]{3,2,1,0:T(8,128)(2,1)S(1)} %get-tuple-element.447), channel_id=1, source_target_pairs={{0,24},{4,28},{8,16},{12,20},{16,8},{20,12},{24,0},{28,4},{1,25},{... | collective-permute-start | bytes 442376 | tf_op jit(solution)/shard_map/ppermute | solution.py:52
  617.5 33.6 %collective-permute-start.91 = (bf16[1,1,96,768]{3,2,1,0:T(8,128)(2,1)S(1)}, bf16[1,1,96,768]{3,2,1,0:T(8,128)(2,1)S(1)}, u32[]{:S(2)}, u32[]{:S(2)}) collective-permute-start(bf16[1,1,96,768]{3,2,1,0:T(8,128)(2,1)S(1)} %get-tuple-element.449), channel_id=1, source_target_pairs={{0,8},{4,12},{8,0},{12,4},{16,24},{20,28},{24,16},{28,20},{1,9},{5... | collective-permute-start | bytes 442376 | tf_op jit(solution)/shard_map/ppermute | solution.py:52
  674.7 53.1 %collective-permute-start.100 = (bf16[1,1,96,768]{3,2,1,0:T(8,128)(2,1)}, bf16[1,1,96,768]{3,2,1,0:T(8,128)(2,1)}, u32[]{:S(2)}, u32[]{:S(2)}) collective-permute-start(bf16[1,1,96,768]{3,2,1,0:T(8,128)(2,1)} %get-tuple-element.444), channel_id=1, source_target_pairs={{0,24},{4,28},{8,16},{12,20},{16,8},{20,12},{24,0},{28,4},{1,25},{... | collective-permute-start | bytes 442376 | tf_op jit(solution)/shard_map/ppermute | solution.py:52
  674.7 53.1 %collective-permute-start.98 = (bf16[1,1,96,768]{3,2,1,0:T(8,128)(2,1)}, bf16[1,1,96,768]{3,2,1,0:T(8,128)(2,1)}, u32[]{:S(2)}, u32[]{:S(2)}) collective-permute-start(bf16[1,1,96,768]{3,2,1,0:T(8,128)(2,1)} %get-tuple-element.443), channel_id=1, source_target_pairs={{0,8},{4,12},{8,0},{12,4},{16,24},{20,28},{24,16},{28,20},{1,9},{5... | collective-permute-start | bytes 442376 | tf_op jit(solution)/shard_map/ppermute | solution.py:52
  (221 other events, 3292.2 us)

commit v2 on v1

v2 whole, which is shorter than its diff:
```python
import functools

import jax
import jax.numpy as jnp
from jax import lax
from jax.experimental import pallas as pl
from jax.experimental.pallas import tpu as pltpu
from jax.sharding import PartitionSpec as P

HD = 64
LW = 20
STEP = 10

lnorm_eps = 1e-12
decay_one = 0.5
decay_two = 0.5
adam_eps = 1e-08
weight_decay = 0.01
rate_in = 0.03
rate_out = 0.1
rate_up = 0.03
rate_down = 0.015
rate_vector = 0.2
rate_bias = 0.2

F32 = jnp.float32
BF16 = jnp.bfloat16
HIGHEST = lax.Precision.HIGHEST

def tie(value, after):
    return lax.optimization_barrier((value, after))[0]


class Plain:
    def __init__(self, mesh):
        self.n_dp, self.n_t = mesh.shape["dp"], mesh.shape["tensor"]
        self.groups = 1

    def row_blocks(self):
        return jnp.arange(self.n_dp, dtype=jnp.int32)

    def piece_at(self, j):
        return jnp.int32(j)

    def gather(self, shard):
        whole = lax.all_gather(shard, "dp", axis=0)[:, None]
        for_all = lax.all_gather(whole, "tensor", axis=0)
        return [[(for_all[j], 0)] for j in range(self.n_t)]

    def first(self, shards):
        return {"a0": self.gather(shards["a0"])}

    def begin(self, pair, shards, after):
        return {name: self.gather(shards[name]) for name in pair}

    def begun(self, state):
        return ()

    def complete(self, state, after):
        return state

    def swap_out(self, stash):
        return list(stash)

    def fold(self, items, after=()):
        stashes, kinds = weight_kinds(items)
        outs = [shape((self.n_t, stashes[0].shape[2], stashes[0].shape[2]), BF16)] * len(items)
        return small(functools.partial(grad_plain_kernel, kinds, self.n_t), stashes, outs, 8, 40, after)

    def send(self, state):
        return state

    def bump(self, state, after=()):
        return state

    def merge(self, state, after=()):
        return state

    def close(self, state):
        out = []
        for full in state:
            mine = lax.psum_scatter(full, "tensor", scatter_dimension=0)
            out.append(lax.psum_scatter(mine, "dp", scatter_dimension=0, tiled=True))
        return out

    def gate(self, state):
        return []

    def first_totals(self, value):
        return lax.psum(value, ("dp", "tensor"))

    def next_total(self, value, axis, after):
        return value


class Grid:
    def __init__(self, mesh):
        self.n_dp, self.n_t = mesh.shape["dp"], mesh.shape["tensor"]
        self.groups = 2
        self.z_groups = [[z * 2 + y for z in range(4)] for y in range(2)]

    def row_blocks(self):
        y = lax.axis_index("dp") % 2
        return jnp.stack([2 * z + (y ^ k) for k in range(2) for z in range(4)])

    def piece_at(self, j):
        return lax.axis_index("tensor") ^ j

    def swap(self, value, axis, mask):
        size = self.n_dp if axis == "dp" else self.n_t
        return lax.ppermute(value, axis, [(i, i ^ mask) for i in range(size)])

    def over_x(self, value):
        return self.swap(value, "tensor", 2)

    def over_core(self, value):
        return self.swap(value, "tensor", 1)

    def over_y(self, value):
        return self.swap(value, "dp", 1)

    def z_gather(self, value):
        z = lax.axis_index("dp") // 2
        out = jnp.zeros((4,) + value.shape, value.dtype)
        out = lax.dynamic_update_slice_in_dim(out, value[None], z, 0)
        for m in range(1, 4):
            out = lax.dynamic_update_slice_in_dim(out, self.swap(value, "dp", 2 * m)[None], z ^ m, 0)
        return out

    def z_scatter(self, value):
        z = lax.axis_index("dp") // 2
        total = lax.dynamic_index_in_dim(value, z, 0, keepdims=False).astype(F32)
        for m in range(1, 4):
            part = lax.dynamic_index_in_dim(value, z ^ m, 0, keepdims=False)
            total = total + self.swap(part, "dp", 2 * m).astype(F32)
        return total.astype(BF16)

    def first(self, shards):
        s = self.z_gather(shards["a0"][None])
        u, t = self.over_x(s), self.over_y(s)
        half = s.shape[-1] // 2
        v = jnp.concatenate([self.over_x(t[..., :half]), self.over_y(u[..., half:])], axis=-1)
        mine = (s, t, u, v)
        other = [self.over_core(k) for k in mine]
        return {"a0": [[(k[0], 0), (k[1], 0)] if j < 2 else [(k[2], 0), (k[3], 0)] for j, k in enumerate((mine, other, mine, other))]}

    def begin(self, pair, shards, after):
        s = lax.all_gather(jnp.stack([shards[n] for n in pair]), "dp", axis=0, axis_index_groups=self.z_groups)
        s = tie(s, after)
        return pair, s, self.over_x(s), self.over_y(s)

    def begun(self, state):
        return state[3:]

    def complete(self, state, after):
        pair, s, u, t = state
        cut_t, cut_u = tie((t, u), after)
        v0, v1 = self.over_x(cut_t[:, 0:1]), self.over_y(cut_u[:, 1:2])
        mine = (s, t, u, v0, v1)
        other = [self.over_core(k) for k in mine]
        out = {}
        for m, name in enumerate(pair):
            out[name] = [
                [(k[0], m), (k[1], m)] if j < 2 else [(k[2], m), (k[3 + m], 0)] for j, k in enumerate((mine, other, mine, other))
            ]
        return out

    def swap_out(self, stash):
        keep, send = stash
        return [keep, self.over_core(send)]

    def fold(self, items, after=()):
        stashes, kinds = weight_kinds(items)
        n, cols = len(items), stashes[0].shape[2]
        half = cols // 2
        cut = cols if n == 2 else cols // 2
        outs = (shape((n, half, cols), BF16),) * 3 + (shape((half, cut), BF16),) * 2
        s, t, u, va, vb = small(functools.partial(grad_kernel, kinds, 2), stashes, outs, 7, 30, after)
        return s, t, u, va, vb

    def send(self, state):
        s, t, u, va, vb = state
        return s, t, u, self.over_x(va), self.over_y(vb)

    def bump(self, state, after=()):
        s, t, u, ra, rb = state
        t, u = tie((t, u), after)
        t, u = small(bump_kernel, [t, u, ra, rb], (shape(t.shape, BF16), shape(u.shape, BF16)), 1.5)
        return s, self.over_y(t), self.over_x(u), t

    def merge(self, state, after=()):
        s, rt, ru, _ = state
        s = tie(s, after)
        n, half, cols = s.shape
        (both,) = small(close_kernel, [s, rt, ru], (shape((4, n, half // 4, cols), BF16),), 1.5)
        return both

    def close(self, both):
        n = both.shape[1]
        if n == 1:
            return [self.z_scatter(both)[0]]
        both = lax.psum_scatter(both, "dp", scatter_dimension=0, axis_index_groups=self.z_groups)
        return [both[i] for i in range(n)]

    def gate(self, state):
        if not isinstance(state, tuple):
            return [state]
        return [state[0] if len(state) == 5 else state[3]]

    def first_totals(self, value):
        for axis, mask in (("tensor", 1), ("dp", 2), ("dp", 4)):
            value = value + self.swap(value, axis, mask)
        return value

    def next_total(self, value, axis, after):
        other = self.over_x(value) if axis == "x" else self.over_y(value)
        return value + tie(other, after)


def adam_step(weight, gradient, first, second, rate):
    first_new = decay_one * first + (1.0 - decay_one) * gradient
    second_new = decay_two * second + (1.0 - decay_two) * gradient * gradient
    fix_one = 1.0 - decay_one**STEP
    fix_two = 1.0 - decay_two**STEP
    ratio = first_new / fix_one / (jnp.sqrt(second_new / fix_two) + adam_eps)
    return (first_new, second_new, weight - rate * (ratio + weight_decay * weight))


def mm(left, right):
    return jnp.dot(left, right, preferred_element_type=F32)


def mm_nt(left, right):
    return lax.dot_general(left, right, (((1,), (1,)), ((), ())), preferred_element_type=F32)


def mm_tn(left, right):
    return lax.dot_general(left, right, (((0,), (0,)), ((), ())), preferred_element_type=F32)


def normed(z, gain, shift):
    centered = z - jnp.mean(z, axis=-1, keepdims=True)
    scale = lax.rsqrt(jnp.mean(centered * centered, axis=-1, keepdims=True) + lnorm_eps)
    xhat = centered * scale
    return xhat * gain + shift, xhat, scale


def norm_back(g, xhat, scale, gain, sums_ref):
    gg = g * gain
    g_z = (gg - jnp.mean(gg, axis=-1, keepdims=True) - xhat * jnp.mean(gg * xhat, axis=-1, keepdims=True)) * scale
    sums_ref[...] = jnp.zeros(sums_ref.shape, F32)
    sums_ref[0:1, :] = jnp.sum(g_z, axis=0, keepdims=True)
    sums_ref[1:2, :] = jnp.sum(g * xhat, axis=0, keepdims=True)
    sums_ref[2:3, :] = jnp.sum(g, axis=0, keepdims=True)
    return g_z


def put_adam(refs, at, gradient, rate):
    w_ref, m_ref, v_ref, g_out, m_out, v_out, w_out, copy_out = refs
    m_new, v_new, w_new = adam_step(w_ref[at], gradient, m_ref[at], v_ref[at], rate)
    g_out[at], m_out[at], v_out[at], w_out[at] = gradient, m_new, v_new, w_new
    copy_out[at] = w_new.astype(BF16)


def adam_ffn_kernel(ins, outs, up_ref, down_ref):
    put_adam(ins[:3] + outs[:5], 0, up_ref[...].astype(F32), rate_up)
    put_adam(ins[3:] + outs[5:], 0, down_ref[...].astype(F32), rate_down)


def adam_att_kernel(ins, outs, share_ref):
    g = share_ref[...].astype(F32)
    cols = ins[0].shape[3]
    for i in range(3):
        put_adam(ins[:3] + outs[:5], (0, i), g[:, i * cols : (i + 1) * cols], rate_in)
    put_adam(ins[3:] + outs[5:], 0, g[:, 3 * cols :].T, rate_out)


def adam_call(kernel, at, shares, groups, earlier):
    flat_in = [a for g in groups for a in g]

    def one(a):
        return pl.BlockSpec((1,) + a.shape[1:], lambda i: at + (0,) * (len(a.shape) - 1))

    outs = []
    for g in groups:
        outs += [shape(g[0].shape)] * 4 + [shape(g[0].shape, BF16)]
    n, n_in, old = len(shares), len(flat_in), list(earlier or ())

    def body(*refs):
        kernel(refs[n : n + n_in], refs[n + n_in + len(old) :], *refs[:n])

    return pl.pallas_call(
        body,
        grid=(1,),
        in_specs=[pl.BlockSpec(a.shape, lambda i: (0, 0)) for a in shares] + [one(a) for a in flat_in] + [pl.BlockSpec(memory_space=pl.ANY)] * len(old),
        out_specs=tuple(one(o) for o in outs),
        out_shape=tuple(outs),
        input_output_aliases={n + n_in + i: i for i in range(len(old))},
        cost_estimate=work(3),
        compiler_params=pltpu.CompilerParams(vmem_limit_bytes=24 * MIB),
    )(*shares, *flat_in, *old)


def head_lanes(hn, width):
    lane = lax.broadcasted_iota(jnp.int32, (1, width), 1) // HD
    return [lane == h for h in range(hn)]


def stacked(value, lanes):
    return jnp.concatenate([jnp.where(m, value, 0.0) for m in lanes], axis=0).astype(BF16)


def gathered(value, lanes):
    rows = value.shape[0] // len(lanes)
    parts = [jnp.where(m, value[h * rows : (h + 1) * rows], 0.0) for h, m in enumerate(lanes)]
    return sum(parts[1:], parts[0])


def probabilities(q_rows, k, mask):
    rows = mask.shape[0]
    s = mm_nt(q_rows, k).reshape(-1, rows, rows) * HD ** (-0.5)
    s = jnp.where(mask[None] > 0, s, -1e30)
    e = jnp.exp(s - jnp.max(s, axis=-1, keepdims=True))
    return (e / jnp.sum(e, axis=-1, keepdims=True)).reshape(-1, rows)


def att_fwd_kernel(n, nw, hn, x_ref, mask_ref, bias_ref, vec_ref, *refs):
    w, (out_ref, xhat_ref, scale_ref, qkv_ref, mix_ref) = split(refs[:nw], n), refs[nw:]
    c, lanes = hn * HD, head_lanes(hn, 256)
    x = x_ref[...]
    x16 = x.astype(BF16)
    z = x + vec_ref[0:1, :]
    for j in range(n):
        qkv = times(x16, w[j]) + bias_ref[j : j + 1, :]
        k = pltpu.roll(qkv[:, c - 64 : c + 192], 192, 1).astype(BF16)
        q, v = qkv[:, :256].astype(BF16), qkv[:, 2 * c : 2 * c + 256].astype(BF16)
        qkv_ref[j, :, :256], qkv_ref[j, :, 256:512], qkv_ref[j, :, 512:] = q, k, v
        p = probabilities(stacked(q.astype(F32), lanes), k, mask_ref[...]).astype(BF16)
        mix = pltpu.roll(gathered(mm(p, v), lanes), 64, 1).astype(BF16)
        mix_ref[j] = mix
        z = z + times_t(mix, w[j], 3 * c - 64)
    out, xhat, scale = normed(z, vec_ref[1:2, :], vec_ref[2:3, :])
    out_ref[...] = out
    xhat_ref[...] = xhat
    scale_ref[...] = jnp.broadcast_to(scale, scale_ref.shape)


def att_bwd_kernel(n, nw, hn, g_ref, x_ref, mask_ref, vec_ref, xhat_ref, scale_ref, qkv_ref, mix_ref, *refs):
    w, (gin_ref, sums_ref, bias_ref), stash = split(refs[:nw], n), refs[nw : nw + 3], refs[nw + 3 :]
    c, lanes, groups = hn * HD, head_lanes(hn, 256), len(stash)
    g_z = norm_back(g_ref[...], xhat_ref[...], scale_ref[:, 0:1], vec_ref[1:2, :], sums_ref)
    wide, x16 = g_z.astype(BF16), x_ref[...].astype(BF16)
    for ref in stash:
        ref[0], ref[1] = x16, wide
    gin = g_z
    for j in range(n):
        q, k, v = qkv_ref[j, :, :256], qkv_ref[j, :, 256:512], qkv_ref[j, :, 512:]
        d_mix = pltpu.roll(times_from(wide, w[j], 3 * c - 64), 192, 1).astype(BF16)
        da, q = stacked(d_mix.astype(F32), lanes), stacked(q.astype(F32), lanes)
        p = probabilities(q, k, mask_ref[...])
        dv = mm_tn(p.astype(BF16), da)
        dp = mm_nt(da, v)
        ds = (p * (dp - jnp.sum(p * dp, axis=-1, keepdims=True))).astype(BF16) * HD ** (-0.5)
        dq = gathered(mm(ds, k), lanes)
        dk = pltpu.roll(mm_tn(ds, q), 64, 1)
        front = [dq[:, :128], dq[:, 128:] + dk[:, :128], dk[:, 128:], dv[:, :128]]
        d_qkv = jnp.concatenate(front + [dv[:, 128:]], axis=1).astype(BF16)
        bias_ref[j : j + 1, :640] = jnp.sum(d_qkv.astype(F32), axis=0, keepdims=True)
        place = stash[j % groups].at[2 + j // groups]
        place[:, :512] = d_qkv[:, :512]
        place[:, 512:640] = d_qkv[:, 512:] + mix_ref[j, :, :128]
        place[:, 640:] = mix_ref[j, :, 128:]
        gin = gin + times_t(d_qkv, w[j], 0, 640)
    gin_ref[...] = gin


def ffn_kernel(n, nw, x_ref, cot_ref, bias_ref, vec_ref, *refs):
    up, down = split(refs[:nw], n), split(refs[nw : 2 * nw], n)
    out_ref, gin_ref, sums_ref, dbias_ref = refs[2 * nw : 2 * nw + 4]
    slope_ref, stash = refs[-1], refs[2 * nw + 4 : -1]
    groups, held = len(stash), n // len(stash)
    x = x_ref[...]
    x16 = x.astype(BF16)
    z = x + vec_ref[0:1, :]
    for j in range(n):
        inner = times(x16, up[j]) + bias_ref[j : j + 1, :]
        half = 0.5 * (1.0 + lax.erf(inner * 0.7071067811865476))
        act = (inner * half).astype(BF16)
        slope_ref[j] = half + inner * (0.3989422804014327 * jnp.exp(-0.5 * inner * inner))
        stash[j % groups][2 + j // groups] = act
        z = z + times_t(act, down[j])
    out, xhat, scale = normed(z, vec_ref[1:2, :], vec_ref[2:3, :])
    out_ref[...] = out
    g_z = norm_back(cot_ref[...].astype(F32), xhat, scale, vec_ref[1:2, :], sums_ref)
    wide = g_z.astype(BF16)
    for ref in stash:
        ref[0], ref[1] = x16, wide
    gin = g_z
    for j in range(n):
        d_inner = (times(wide, down[j]) * slope_ref[j]).astype(BF16)
        dbias_ref[j : j + 1, :] = jnp.sum(d_inner.astype(F32), axis=0, keepdims=True)
        stash[j % groups][2 + held + j // groups] = d_inner
        gin = gin + times_t(d_inner, up[j])
    gin_ref[...] = gin


def weight_grad(kind, refs, i, held):
    total = None
    for ref in refs:
        if kind == "d":
            part = mm_tn(ref[1], ref[2 + i])
        elif kind == "u":
            part = mm_tn(ref[0], ref[2 + held + i])
        else:
            both = ref[2 + i]
            part = mm_tn(ref[0], both)
            tail = mm_tn(ref[1], both[:, 512:])
            own = lax.broadcasted_iota(jnp.int32, (1, 256), 1) < 64
            part = jnp.concatenate([part[:, :512], jnp.where(own, part[:, 512:], tail)], axis=1)
        total = part if total is None else total + part
    return total.astype(BF16)


def grad_kernel(kinds, held, *refs):
    outs = refs[-5:]
    s_ref, t_ref, u_ref, va_ref, vb_ref = outs
    for m, (kind, at) in enumerate(kinds):
        g = weight_grad(kind, [refs[i] for i in at], 1, held)
        half = g.shape[0] // 2
        u_ref[m], v = g[:half], g[half:]
        if len(kinds) == 1:
            va_ref[...], vb_ref[...] = v[:, : v.shape[1] // 2], v[:, v.shape[1] // 2 :]
        elif m == 0:
            va_ref[...] = v
        else:
            vb_ref[...] = v
        g = weight_grad(kind, [refs[i] for i in at], 0, held)
        s_ref[m], t_ref[m] = g[:half], g[half:]


def grad_plain_kernel(kinds, held, *refs):
    for m, (kind, at) in enumerate(kinds):
        for i in range(held):
            refs[len(refs) - len(kinds) + m][i] = weight_grad(kind, [refs[k] for k in at], i, held)


def bump_kernel(t_ref, u_ref, a_ref, b_ref, t_out, u_out):
    cut, cols, last = a_ref.shape[1], t_ref.shape[2], u_ref.shape[0] - 1
    t_out[...] = t_ref[...]
    u_out[...] = u_ref[...]
    t_out[0, :, :cut] = (t_ref[0, :, :cut].astype(F32) + a_ref[...].astype(F32)).astype(BF16)
    u_out[last, :, cols - cut :] = (u_ref[last, :, cols - cut :].astype(F32) + b_ref[...].astype(F32)).astype(BF16)


def close_kernel(s_ref, t_ref, u_ref, out_ref):
    n, rows = s_ref.shape[0], s_ref.shape[1] // 4
    for m in range(n):
        for z in range(4):
            at = slice(z * rows, (z + 1) * rows)
            out_ref[z, m] = (s_ref[m, at].astype(F32) + t_ref[m, at].astype(F32) + u_ref[m, at].astype(F32)).astype(BF16)


def small(kernel, args, outs, micros, limit=24, after=()):
    vmem, n_in = pl.BlockSpec(memory_space=pltpu.VMEM), len(args)

    def body(*refs):
        kernel(*refs[:n_in], *refs[n_in + len(after) :])

    return pl.pallas_call(
        body,
        in_specs=[vmem] * n_in + [pl.BlockSpec(memory_space=pl.ANY)] * len(after),
        out_specs=tuple([vmem] * len(outs)),
        out_shape=tuple(outs),
        cost_estimate=work(micros),
        compiler_params=pltpu.CompilerParams(vmem_limit_bytes=limit * MIB),
    )(*args, *after)


def flat(ref):
    k, _, r, c = ref.shape
    return ref[...].reshape(k * r, c)


def times(x, refs):
    total, at = None, 0
    for ref in refs:
        w = flat(ref)
        part = mm(x[:, at : at + w.shape[0]], w)
        total = part if total is None else total + part
        at += w.shape[0]
    return total


def times_t(x, refs, start=0, stop=None):
    return jnp.concatenate([mm_nt(x, flat(ref)[:, start:stop]) for ref in refs], axis=1)


def times_from(x, refs, start):
    total, at = None, 0
    for ref in refs:
        w = flat(ref)[:, start:]
        part = mm(x[:, at : at + w.shape[0]], w)
        total = part if total is None else total + part
        at += w.shape[0]
    return total


def split(refs, n):
    size = len(refs) // n
    return [refs[i * size : (i + 1) * size] for i in range(n)]


MIB = 1024 * 1024


def work(micros):
    return pl.CostEstimate(flops=int(micros * 1.1e9), bytes_accessed=1024, transcendentals=0)


def call(kernel, args, weights, outs, cost, vmem, after=(), scratch=()):
    chunks = [c for piece in weights for c in piece]
    n_in, waits = len(args) + len(chunks), len(after)

    def body(*refs):
        kernel(*refs[:n_in], *refs[n_in + waits :])

    once = pl.Buffered(buffer_count=1)

    def whole(a):
        return pl.BlockSpec(a.shape, lambda i, nd=len(a.shape): (0,) * nd, pipeline_mode=once)

    def picked(a, m):
        k, _, r, c = a.shape
        return pl.BlockSpec((k, 1, r, c), lambda i: (0, m, 0, 0), pipeline_mode=once)

    return pl.pallas_call(
        body,
        grid=(1,),
        out_shape=tuple(outs),
        scratch_shapes=list(scratch),
        in_specs=[whole(a) for a in args] + [picked(a, m) for a, m in chunks]
        + [pl.BlockSpec(memory_space=pl.ANY)] * waits,
        out_specs=tuple(whole(o) for o in outs),
        compiler_params=pltpu.CompilerParams(vmem_limit_bytes=vmem * MIB),
        cost_estimate=cost,
    )(*args, *[a for a, m in chunks], *after)


def shape(dims, kind=F32):
    return jax.ShapeDtypeStruct(dims, kind)


def dims_of(piece):
    return [a.shape[0] * a.shape[2] for a, m in piece], piece[0][0].shape[3]


def count(w):
    return len(w), sum(len(p) for p in w)


def att_forward(x, mask, bias, vec, w, hn):
    (n, nw), (rows, width) = count(w), x.shape
    outs = [shape((rows, width)), shape((rows, width)), shape((rows, 128)), shape((n, rows, 768), BF16), shape((n, rows, 256), BF16)]
    return call(functools.partial(att_fwd_kernel, n, nw, hn), [x, mask, bias, vec], w, outs, work(4 + rows / 50), 30)


def att_backward(g, x, mask, vec, kept, w, hn, groups, after=()):
    (n, nw), (rows, width) = count(w), x.shape
    outs = [shape((rows, width)), shape((8, width)), shape((n, dims_of(w[0])[1]))] + [shape((2 + n // groups, rows, width), BF16)] * groups
    res = call(functools.partial(att_bwd_kernel, n, nw, hn), [g, x, mask, vec] + list(kept), w, outs, work(5 + rows / 30), 30, after)
    return res[0], res[1], res[2], res[3:]


def ffn_both(x, cot, bias, vec, up, down, groups, after=()):
    (n, nw), (rows, width), f = count(up), x.shape, dims_of(up[0])[1]
    outs = [shape((rows, width)), shape((rows, width)), shape((8, width)), shape((n, f))]
    outs += [shape((2 + 2 * n // groups, rows, width), BF16)] * groups
    scratch = [pltpu.VMEM((n, rows, f), F32)]
    res = call(functools.partial(ffn_kernel, n, nw), [x, cot, bias, vec], up + down, outs, work(5 + rows / 30), 38, after, scratch)
    return res[0], res[1], res[2], res[3], res[4:]


def weight_kinds(items):
    stashes = []
    kinds = []
    for kind, arrays in items:
        at = []
        for array in arrays:
            same = [i for i, s in enumerate(stashes) if s is array]
            at.append(same[0] if same else len(stashes))
            stashes += [] if same else [array]
        kinds.append((kind, tuple(at)))
    return stashes, tuple(kinds)


def make_local(mesh):
    n_t = mesh.shape["tensor"]
    net = (Grid if (mesh.shape["dp"], n_t) == (8, 4) else Plain)(mesh)

    def local(
        lang_in, visn_in, word_len, lang_cot, visn_cot, att_in, att_out, ffn_up, ffn_down, vectors, ffn_bias1,
        att_in_m, att_in_v, att_out_m, att_out_v, ffn_up_m, ffn_up_v, ffn_down_m, ffn_down_v,
        vectors_m, vectors_v, bias1_m, bias1_v,
    ):
        width = lang_in.shape[1]
        rows = att_in.shape[1]
        cols = att_in.shape[3]
        ff = ffn_up.shape[2]
        heads_here = cols // HD
        items = word_len.shape[0]
        usable = jnp.arange(LW, dtype=jnp.int32)[None, :] < word_len[:, None]

        shards = {}
        for b in range(3):
            shards["a%d" % b] = jnp.concatenate(
                [att_in[b].astype(BF16).reshape(rows, 3 * cols), att_out[b].astype(BF16).T], axis=1
            )
        for i in range(2):
            shards["u%d" % i] = ffn_up[i].astype(BF16)
            shards["d%d" % i] = ffn_down[i].astype(BF16).T

        index_of = (net.row_blocks()[:, None] * rows + jnp.arange(rows, dtype=jnp.int32)[None, :]).reshape(-1)
        turn = (jnp.arange(width, dtype=jnp.int32)[:, None] == index_of[None, :])
        turn16, turn32 = turn.astype(BF16), turn.astype(F32)

        def to_rel(value):
            return mm(value, turn16).astype(BF16)

        def to_abs(value):
            return lax.dot_general(value, turn32, (((1,), (1,)), ((), ())), precision=HIGHEST)

        def by_piece(value, axis):
            return jnp.stack([lax.dynamic_index_in_dim(value, net.piece_at(j), axis, keepdims=False) for j in range(n_t)], axis=axis)

        vec = jnp.dot(vectors, turn32, precision=HIGHEST)
        vec_heads = by_piece(vectors.reshape(-1, n_t, cols), 1)
        bias_ff = by_piece(ffn_bias1.reshape(2, n_t, ff), 1)

        qv = jnp.zeros((3, n_t, 4 * cols), F32)
        for b in range(3):
            qv = qv.at[b, :, :cols].set(vec_heads[5 * b]).at[b, :, 2 * cols : 3 * cols].set(vec_heads[5 * b + 1])

        def rows3(row):
            return vec[row : row + 3]

        n_lang, n_visn = lang_in.shape[0], visn_in.shape[0]
        slots, regions = n_lang // items, n_visn // items
        item = jnp.concatenate([jnp.arange(n_lang) // slots, jnp.arange(n_visn) // regions])
        is_lang = jnp.arange(n_lang + n_visn) < n_lang
        seen = jnp.concatenate([usable.reshape(-1), jnp.ones((n_visn,), bool)])
        same = (item[:, None] == item[None, :]) & seen[None, :]
        mask0 = (same & (is_lang[:, None] != is_lang[None, :])).astype(F32)
        mask1 = same[:n_lang, :n_lang].astype(F32)
        mask2 = same[n_lang:, n_lang:].astype(F32)

        x0 = to_rel(jnp.concatenate([lang_in, visn_in], axis=0)).astype(F32)
        full = net.first(shards)
        later = tie({k: v for k, v in shards.items() if k != "a0"}, shards["a0"])
        pair1 = net.begin(("a1", "a2"), later, ())
        both1, *kept0 = att_forward(x0, mask0, qv[0], rows3(2), full["a0"], heads_here)
        full.update(net.complete(pair1, both1))
        pair2 = net.begin(("u0", "d0"), later, net.begun(pair1))
        lang1, visn1 = both1[:n_lang], both1[n_lang:]
        lang2, *kept1 = att_forward(lang1, mask1, qv[1], rows3(7), full["a1"], heads_here)
        visn2, *kept2 = att_forward(visn1, mask2, qv[2], rows3(12), full["a2"], heads_here)
        full.update(net.complete(pair2, (lang2, visn2)))
        pair3 = net.begin(("u1", "d1"), later, net.begun(pair2))
        groups = net.groups
        lang_out, g_lang, sums15, bias_lang, stash = ffn_both(lang2, to_rel(lang_cot), bias_ff[0], rows3(15), full["u0"], full["d0"], groups)
        full.update(net.complete(pair3, lang_out))
        rows_f0 = net.swap_out(stash)
        g_lang, sums7, bias1, stash = att_backward(g_lang, lang1, mask1, rows3(7), kept1, full["a1"], heads_here, groups)
        rows_a1 = net.swap_out(stash)
        part0 = net.send(net.fold([("d", rows_f0), ("u", rows_f0)], [sums7]))
        first = ffn_both(visn2, to_rel(visn_cot), bias_ff[1], rows3(18), full["u1"], full["d1"], groups, net.gate(part0))
        part0 = net.bump(part0, first[2])
        visn_out, g_visn, sums18, bias_visn, stash = tie(first, net.gate(part0))
        rows_f1 = net.swap_out(stash)
        g_visn, sums12, bias2, stash = att_backward(g_visn, visn1, mask2, rows3(12), kept2, full["a2"], heads_here, groups, net.gate(part0))
        rows_a2 = net.swap_out(stash)
        part1 = net.send(net.fold([("d", rows_f1), ("u", rows_f1)], [sums12]))
        part2 = net.send(net.fold([("a", rows_a1), ("a", rows_a2)], net.gate(part1)))
        part0 = net.merge(part0, net.gate(part2))
        share0 = net.close(part0)
        first = att_backward(
            jnp.concatenate([g_lang, g_visn], axis=0), x0, mask0, rows3(2), kept0, full["a0"], heads_here, groups, net.gate(part2) + net.gate(part0)
        )
        part1, part2 = net.bump(part1, first[1]), net.bump(part2, first[1])
        g_both, sums2, bias0, stash = tie(first, net.gate(part1) + net.gate(part2))
        rows_a0 = net.swap_out(stash)
        part3 = net.send(net.fold([("a", rows_a0)], net.gate(part2)))
        part1 = net.merge(part1, net.gate(part3))
        share1 = net.close(part1)
        part2 = net.merge(part2, net.gate(part1))
        share2 = net.close(part2)

        t_in, t_in_m, t_in_v = (jnp.transpose(k, (0, 2, 1, 3)) for k in (att_in, att_in_m, att_in_v))
        up_all = (ffn_up, ffn_up_m, ffn_up_v)
        down_all = [jnp.transpose(k, (0, 2, 1)) for k in (ffn_down, ffn_down_m, ffn_down_v)]
        ffn_new = adam_call(adam_ffn_kernel, (0,), share0[1::-1], [up_all, down_all], None)
        ffn_new = adam_call(adam_ffn_kernel, (1,), share1[1::-1], [up_all, down_all], ffn_new)
        blank = jnp.zeros((2, width), F32)
        by_rows = to_abs(jnp.concatenate([blank, sums2[:3], blank, sums7[:3], blank, sums12[:3], sums15[:3], sums18[:3]], axis=0))
        hrows = {}
        for b, value in enumerate((bias0, bias1, bias2)):
            hrows[5 * b], hrows[5 * b + 1] = value[:, :cols], value[:, 2 * cols : 3 * cols]
        out_abs = to_abs(jnp.concatenate([lang_out, visn_out, g_both], axis=0))
        n_both = n_lang + n_visn
        lang_out, visn_out = out_abs[:n_lang], out_abs[n_lang:n_both]
        lang_grad, visn_grad = out_abs[n_both : n_both + n_lang], out_abs[n_both + n_lang :]

        for row, value in hrows.items():
            by_rows = by_rows.at[row].set(by_piece(value, 0).reshape(-1))
        bias_all = by_piece(jnp.stack([bias_lang, bias_visn]), 1)
        sums = net.first_totals(tie(jnp.concatenate([by_rows, bias_all.reshape(-1, width)], axis=0), net.gate(part2)))
        part3 = net.bump(part3)
        sums = net.next_total(sums, "x", net.gate(part3))
        part3 = net.merge(part3, ffn_new[0])
        sums = net.next_total(sums, "y", net.gate(part3))
        share3 = net.close(part3)
        vector_grad, bias1_grad = sums[:21], sums[21:].reshape(ffn_bias1.shape)

        att_all = [(t_in, t_in_m, t_in_v), (att_out, att_out_m, att_out_v)]
        att_new = adam_call(adam_att_kernel, (1,), share2[:1], att_all, None)
        att_new = adam_call(adam_att_kernel, (2,), share2[1:], att_all, att_new)
        att_new = adam_call(adam_att_kernel, (0,), share3, att_all, att_new)
        in_new = [jnp.transpose(k, (0, 2, 1, 3)) for k in att_new[:5]]

        result = [lang_out, visn_out, lang_grad, visn_grad] + in_new + list(att_new[5:]) + list(ffn_new[:5]) + [jnp.transpose(k, (0, 2, 1)) for k in ffn_new[5:]]
        for share, weight, first, second, rate in (
            (vector_grad, vectors, vectors_m, vectors_v, rate_vector),
            (bias1_grad, ffn_bias1, bias1_m, bias1_v, rate_bias),
        ):
            m_new, v_new, w_new = adam_step(weight, share, first, second, rate)
            result += [share, m_new, v_new, w_new]
        return tuple(result)

    return local


def solution(mesh):
    rows = P(("dp", "tensor"), None)
    w_in, w_out, w_up, w_down = P(None, "dp", None, "tensor"), P(None, "tensor", "dp"), P(None, "dp", "tensor"), P(None, "tensor", "dp")
    return jax.shard_map(
        make_local(mesh),
        mesh=mesh,
        in_specs=(rows, rows, P(("dp", "tensor")), rows, rows, w_in, w_out, w_up, w_down, P(), P())
        + (w_in,) * 2 + (w_out,) * 2 + (w_up,) * 2 + (w_down,) * 2 + (P(),) * 4,
        out_specs=(rows,) * 4 + (w_in,) * 5 + (w_out,) * 5 + (w_up,) * 5 + (w_down,) * 5 + (P(),) * 8,
        check_vma=False,
    )
```

time: 740 us -> 449 us (0.61)
  starting transfers between devices: 209 us -> 61.4 us
  waiting for transfers between devices: 241 us -> 165 us
  other arithmetic: 64.4 us -> 16.6 us
  local copies, waits for them, and re-layouts: 80.9 us -> 56.4 us
  between operations: 3.09 us -> 16 us
    ppermute x118 -> x67, starting transfers between devices: 209 us -> 60.9 us  [swap(): return lax.ppermute(value, axis, [(i, i ^ mask) for i in range(size)])]
    ppermute x118 -> x67, waiting for transfers between devices: 241 us -> 165 us  [swap(): return lax.ppermute(value, axis, [(i, i ^ mask) for i in range(size)])]
    concatenate x15 -> x2, other arithmetic: 25.5 us -> 0.08 us  [local(): jnp.concatenate([att_in[b].astype(BF16).reshape(rows, 3 * cols), att_out[...]
    convert_element_type x32 -> x0, other arithmetic: 25.4 us -> none  [the longest x26 17 us: scatter(): new[j] = total.astype(BF16)]
    concatenate x10 -> x1, local copies, waits for them, and re-layouts: 13.4 us -> 0.74 us  [first(): jnp.concatenate([self.over_x(t[..., :half]), self.over_y(u[..., half:])],...]
    pallas_call x12 -> x25, Pallas kernels: 124 us -> 118 us  [the longest x8 80.6 us: call(): pl.pallas_call(body, grid=(1,), out_shape=tuple(outs), scratch_shapes=lis...]
    unnamed x290 -> x228, local copies, waits for them, and re-layouts: 36.6 us -> 34.3 us
  transfers between devices with their start and end apart: 118 -> 73, of which waited for: 34 -> 26; matrix products, arithmetic and copies ran while one was open for 19% -> 10% of each run, Pallas kernels for 9% -> 26%
where the time goes in v2:
time: 449 us; the launch traced here: 444 us
  waiting for transfers between devices  165 us (37%)
  Pallas kernels  118 us (26%)
  starting transfers between devices  61.4 us (14%)
  local copies, waits for them, and re-layouts  56.4 us (13%)
  other arithmetic  16.6 us (4%)
  between operations  16 us (4%)
  matrix products  10.4 us (2%)
    ppermute x67, waiting for transfers between devices, swap(): return lax.ppermute(value, axis, [(i, i ^ mask) for i in range(size)])  165 us
    pallas_call x8, Pallas kernels, call(): pl.pallas_call(body, grid=(1,), out_shape=tuple(outs), scratch_shapes=lis...  80.6 us
    ppermute x67, starting transfers between devices, swap(): return lax.ppermute(value, axis, [(i, i ^ mask) for i in range(size)])  60.9 us
    unnamed x228, local copies, waits for them, and re-layouts  34.3 us
    pallas_call x12, Pallas kernels, small(): pl.pallas_call(body, in_specs=[vmem] * n_in + [pl.BlockSpec(memory_space=...  29.9 us
  transfers between devices with their start and end apart: 73, of which 26 were waited for; matrix products, arithmetic and copies ran while one was open for 10% of the time, Pallas kernels for 26%

profile of v2, /device:TPU:0, one launch (start us, length us, event | category | flops | bytes accessed | tf_op | source)
XLA Modules:
  0.0 444.1 jit_solution(4850146060308119650)
XLA Ops:
  11.6 3.1 collective-permute-start
  23.3 10.0 %collective-permute-done.1 = bf16[1,96,768]{2,1,0:T(8,128)(2,1)S(1)} collective-permute-done((bf16[1,96,768]{2,1,0:T(8,128)(2,1)S(1)}, bf16[1,96,768]{2,1,0:T(8,128)(2,1)S(1)}, u32[]{:S(2)}, u32[]{:S(2)}) %collective-permute-start.1) | collective-permute-done | bytes 147488 | tf_op jit(solution)/shard_map/ppermute | solution.py:111
  39.1 6.3 %collective-permute-done.3.refs_5_.refs_9_ = bf16[4,1,96,768]{3,2,1,0:T(8,128)(2,1)S(1)} collective-permute-done((bf16[4,1,96,768]{3,2,1,0:T(8,128)(2,1)S(1)}, bf16[4,1,96,768]{3,2,1,0:T(8,128)(2,1)S(1)}, u32[]{:S(2)}, u32[]{:S(2)}) %collective-permute-start.3) | collective-permute-done | bytes 589856 | tf_op jit(solution)/shard_map/ppermute | solution.py:111
  63.5 11.2 %shard_map.470 = (f32[336,768]{1,0:T(8,128)S(1)}, f32[336,768]{1,0:T(8,128)S(1)}, f32[336,128]{1,0:T(8,128)S(1)}, bf16[4,336,768]{2,1,0:T(8,128)(2,1)S(1)}, bf16[4,336,256]{2,1,0:T(8,128)(2,1)S(1)}) custom-call(f32[336,768]{1,0:T(8,128)S(1)} %copy-done.42, f32[336,336]{1,0:T(8,128)S(1)} %get-tuple-element.585.refs_1_.refs_2_, ...), custom_call_target="tpu_custom_call" | custom-call | flops 11792000000 | bytes 1024 | tf_op jit(solution)/shard_map/pallas_call | solution.py:536
  76.8 11.5 %collective-permute-done.11.refs_5_.refs_9_ = bf16[4,2,96,768]{3,2,1,0:T(8,128)(2,1)} collective-permute-done((bf16[4,2,96,768]{3,2,1,0:T(8,128)(2,1)}, bf16[4,2,96,768]{3,2,1,0:T(8,128)(2,1)}, u32[]{:S(2)}, u32[]{:S(2)}) %collective-permute-start.11) | collective-permute-done | bytes 1179680 | tf_op jit(solution)/shard_map/ppermute | solution.py:111
  94.0 11.5 %collective-permute-done.22.refs_9_.refs_13_ = bf16[4,1,96,768]{3,2,1,0:T(8,128)(2,1)} collective-permute-done((bf16[4,1,96,768]{3,2,1,0:T(8,128)(2,1)S(1)}, bf16[4,1,96,768]{3,2,1,0:T(8,128)(2,1)}, u32[]{:S(2)}, u32[]{:S(2)}) %collective-permute-start.22) | collective-permute-done | bytes 589856 | tf_op jit(solution)/shard_map/ppermute | solution.py:111
  112.4 8.1 %shard_map.472 = (f32[216,768]{1,0:T(8,128)S(1)}, f32[216,768]{1,0:T(8,128)S(1)}, f32[216,128]{1,0:T(8,128)S(1)}, bf16[4,216,768]{2,1,0:T(8,128)(2,1)S(1)}, bf16[4,216,256]{2,1,0:T(8,128)(2,1)S(1)}) custom-call(f32[216,768]{1,0:T(8,128)S(1)} %slice.476.refs_0_.refs_1_, f32[216,216]{1,0:T(8,128)S(1)} %copy-done.9, f32[4,768]{1,0:T(4,128)S(1)} %get-tuple-element.542.refs_2_, ...), custom_call_target="tpu_custom_call" | custom-call | flops 9152000000 | bytes 1024 | tf_op jit(solution)/shard_map/pallas_call | solution.py:536
  123.0 7.4 %shard_map.471 = (f32[120,768]{1,0:T(8,128)S(1)}, f32[120,768]{1,0:T(8,128)S(1)}, f32[120,128]{1,0:T(8,128)S(1)}, bf16[4,120,768]{2,1,0:T(8,128)(2,1)S(1)}, bf16[4,120,256]{2,1,0:T(8,128)(2,1)S(1)}) custom-call(f32[120,768]{1,0:T(8,128)S(1)} %slice.461.refs_0_.refs_1_, f32[120,120]{1,0:T(8,128)S(1)} %copy-done.16, f32[4,768]{1,0:T(4,128)S(1)} %get-tuple-element.541.refs_2_, ...), custom_call_target="tpu_custom_call" | custom-call | flops 7040000000 | bytes 1024 | tf_op jit(solution)/shard_map/pallas_call | solution.py:536
  130.5 8.0 %collective-permute-done.18.refs_5_.refs_13_ = bf16[4,2,96,768]{3,2,1,0:T(8,128)(2,1)} collective-permute-done((bf16[4,2,96,768]{3,2,1,0:T(8,128)(2,1)}, bf16[4,2,96,768]{3,2,1,0:T(8,128)(2,1)}, u32[]{:S(2)}, u32[]{:S(2)}) %collective-permute-start.18) | collective-permute-done | bytes 1179680 | tf_op jit(solution)/shard_map/ppermute | solution.py:111
  144.6 10.2 %collective-permute-done.24.refs_9_ = bf16[4,1,96,768]{3,2,1,0:T(8,128)(2,1)} collective-permute-done((bf16[4,1,96,768]{3,2,1,0:T(8,128)(2,1)S(1)}, bf16[4,1,96,768]{3,2,1,0:T(8,128)(2,1)}, u32[]{:S(2)}, u32[]{:S(2)}) %collective-permute-start.24) | collective-permute-done | bytes 589856 | tf_op jit(solution)/shard_map/ppermute | solution.py:111
  162.0 9.8 %shard_map.473 = (f32[120,768]{1,0:T(8,128)S(1)}, f32[120,768]{1,0:T(8,128)S(1)}, f32[8,768]{1,0:T(8,128)S(1)}, f32[4,768]{1,0:T(4,128)S(1)}, bf16[6,120,768]{2,...) custom-call(f32[120,768]{1,0:T(8,128)S(1)} %copy-done.82, bf16[120,768]{1,0:T(8,128)(2,1)S(1)} %fusion.22.refs_1_, ...), custom_call_target="tpu_custom_call" | custom-call | flops 9900000256 | bytes 1024 | tf_op jit(solution)/shard_map/pallas_call | solution.py:536
  171.8 14.3 %collective-permute-done.29.refs_5_.refs_13_ = bf16[4,2,96,768]{3,2,1,0:T(8,128)(2,1)S(1)} collective-permute-done((bf16[4,2,96,768]{3,2,1,0:T(8,128)(2,1)}, bf16[4,2,96,768]{3,2,1,0:T(8,128)(2,1)S(1)}, u32[]{:S(2)}, u32[]{:S(2)}) %collective-permute-start.29) | collective-permute-done | bytes 1179680 | tf_op jit(solution)/shard_map/ppermute | solution.py:111
  190.8 11.2 %collective-permute-done.33.refs_9_ = bf16[4,1,96,768]{3,2,1,0:T(8,128)(2,1)S(1)} collective-permute-done((bf16[4,1,96,768]{3,2,1,0:T(8,128)(2,1)S(1)}, bf16[4,1,96,768]{3,2,1,0:T(8,128)(2,1)S(1)}, u32[]{:S(2)}, u32[]{:S(2)}) %collective-permute-start.33) | collective-permute-done | bytes 589856 | tf_op jit(solution)/shard_map/ppermute | solution.py:111
  202.1 7.6 %shard_map.474 = (f32[120,768]{1,0:T(8,128)S(1)}, f32[8,768]{1,0:T(8,128)S(1)}, f32[4,768]{1,0:T(4,128)S(1)}, bf16[4,120,768]{2,1,0:T(8,128)(2,1)S(1)}, bf16[4,120,768]{2,1,0:T(8,128)(2,1)S(1)}) custom-call(f32[120,768]{1,0:T(8,128)S(1)} %get-tuple-element.356.refs_0_, f32[120,768]{1,0:T(8,128)S(1)} %slice.461.refs_0_.refs_1_, f32[120,120]{1,0:T(8,128)S(1)} %copy-done.16, ...), custom_call_target="tpu_custom_call" | custom-call | flops 9900000256 | bytes 1024 | tf_op jit(solution)/shard_map/pallas_call | solution.py:536
  210.4 2.6 shard_map.475
  215.1 9.7 %shard_map.476 = (f32[216,768]{1,0:T(8,128)S(1)}, f32[216,768]{1,0:T(8,128)S(1)}, f32[8,768]{1,0:T(8,128)S(1)}, f32[4,768]{1,0:T(4,128)S(1)}, bf16[6,216,768]{2,...) custom-call(f32[216,768]{1,0:T(8,128)S(1)} %copy-done.86, bf16[216,768]{1,0:T(8,128)(2,1)S(1)} %fusion.14.refs_1_, ...), custom_call_target="tpu_custom_call" | custom-call | flops 13420000256 | bytes 1024 | tf_op jit(solution)/shard_map/pallas_call | solution.py:536
  230.4 9.6 %shard_map.478 = (f32[216,768]{1,0:T(8,128)S(1)}, f32[8,768]{1,0:T(8,128)S(1)}, f32[4,768]{1,0:T(4,128)S(1)}, bf16[4,216,768]{2,1,0:T(8,128)(2,1)S(1)}, bf16[4,216,768]{2,1,0:T(8,128)(2,1)S(1)}) custom-call(f32[216,768]{1,0:T(8,128)S(1)} %get-tuple-element.378.refs_0_, f32[216,768]{1,0:T(8,128)S(1)} %slice.476.refs_0_.refs_1_, f32[216,216]{1,0:T(8,128)S(1)} %copy-done.10, ...), custom_call_target="tpu_custom_call" | custom-call | flops 13420000256 | bytes 1024 | tf_op jit(solution)/shard_map/pallas_call | solution.py:536
  241.9 3.7 shard_map.479
  245.7 4.1 shard_map.480
  256.3 13.1 %collective-permute-done.44.refs_1_ = bf16[2,384,768]{2,1,0:T(8,128)(2,1)S(1)} collective-permute-done((bf16[2,384,768]{2,1,0:T(8,128)(2,1)S(1)}, bf16[2,384,768]{2,1,0:T(8,128)(2,1)S(1)}, u32[]{:S(2)}, u32[]{:S(2)}) %collective-permute-start.44) | collective-permute-done | bytes 1179680 | tf_op jit(solution)/shard_map/ppermute | solution.py:111
  278.9 17.2 %shard_map.482 = (f32[336,768]{1,0:T(8,128)S(1)}, f32[8,768]{1,0:T(8,128)S(1)}, f32[4,768]{1,0:T(4,128)S(1)}, bf16[4,336,768]{2,1,0:T(8,128)(2,1)S(1)}, bf16[4,336,768]{2,1,0:T(8,128)(2,1)}) custom-call(f32[336,768]{1,0:T(8,128)S(1)} %pad_maximum_fusion.refs_0_, f32[336,768]{1,0:T(8,128)S(1)} %copy-done.43, ...), custom_call_target="tpu_custom_call" | custom-call | flops 17820000256 | bytes 1024 | tf_op jit(solution)/shard_map/pallas_call | solution.py:536
  296.2 2.7 shard_map.484
  311.2 3.5 shard_map.485
  317.1 15.8 %collective-permute-done.51.refs_1_ = bf16[2,384,768]{2,1,0:T(8,128)(2,1)} collective-permute-done((bf16[2,384,768]{2,1,0:T(8,128)(2,1)}, bf16[2,384,768]{2,1,0:T(8,128)(2,1)}, u32[]{:S(2)}, u32[]{:S(2)}) %collective-permute-start.51) | collective-permute-done | bytes 1179680 | tf_op jit(solution)/shard_map/ppermute | solution.py:111
  334.1 3.2 shard_map.486
  341.6 5.6 %fusion.1 = f32[672,768]{1,0:T(8,128)} fusion(f32[336,768]{1,0:T(8,128)} %copy-done.49, f32[216,768]{1,0:T(8,128)S(1)} %copy-done.51, f32[120,768]{1,0:T(8,128)} %copy-done.52, s32[768]{0:T(1024)S(1)} %add.205), kind=kOutput, calls=%fused_computation.2 | convolution fusion | flops 4757962752 | bytes 4131840 | tf_op jit(solution)/shard_map/dot_general | solution.py:630
  347.2 17.9 %collective-permute-done.60.refs_1_ = bf16[2,384,768]{2,1,0:T(8,128)(2,1)} collective-permute-done((bf16[2,384,768]{2,1,0:T(8,128)(2,1)S(1)}, bf16[2,384,768]{2,1,0:T(8,128)(2,1)}, u32[]{:S(2)}, u32[]{:S(2)}) %collective-permute-start.60) | collective-permute-done | bytes 1179680 | tf_op jit(solution)/shard_map/ppermute | solution.py:111
  365.9 3.1 shard_map.491
  371.8 7.3 %collective-permute-start.63 = (f32[29,768]{1,0:T(8,128)S(1)}, f32[29,768]{1,0:T(8,128)S(1)}, u32[]{:S(2)}, u32[]{:S(2)}) collective-permute-start(f32[29,768]{1,0:T(8,128)S(1)} %add.217), channel_id=1, source_target_pairs={{0,8},{4,12},{8,0},{12,4},{16,24},{20,28},{24,16},{28,20},{1,9},{5... | collective-permute-start | bytes 267272 | tf_op jit(solution)/shard_map/ppermute | solution.py:111
  382.0 4.7 %collective-permute-start.64 = (f32[29,768]{1,0:T(8,128)S(1)}, f32[29,768]{1,0:T(8,128)S(1)}, u32[]{:S(2)}, u32[]{:S(2)}) collective-permute-start(f32[29,768]{1,0:T(8,128)S(1)} %add.218), channel_id=1, source_target_pairs={{0,16},{4,20},{8,24},{12,28},{16,0},{20,4},{24,8},{28,12},{1,17},{... | collective-permute-start | bytes 267272 | tf_op jit(solution)/shard_map/ppermute | solution.py:111
  387.7 9.4 %collective-permute-done.64 = f32[29,768]{1,0:T(8,128)S(1)} collective-permute-done((f32[29,768]{1,0:T(8,128)S(1)}, f32[29,768]{1,0:T(8,128)S(1)}, u32[]{:S(2)}, u32[]{:S(2)}) %collective-permute-start.64) | collective-permute-done | bytes 89120 | tf_op jit(solution)/shard_map/ppermute | solution.py:111
  411.0 7.7 %collective-permute-done.55.refs_1_ = bf16[1,384,768]{2,1,0:T(8,128)(2,1)} collective-permute-done((bf16[1,384,768]{2,1,0:T(8,128)(2,1)}, bf16[1,384,768]{2,1,0:T(8,128)(2,1)}, u32[]{:S(2)}, u32[]{:S(2)}) %collective-permute-start.55) | collective-permute-done | bytes 589856 | tf_op jit(solution)/shard_map/ppermute | solution.py:111
  (499 shorter events, 157.1 us)
Async XLA Ops:
  7.2 52.5 %all-gather.7.cloned.1.call-start = ((), (), s32[]{:S(2)}) async-start(), calls=%async_computation.6 | async-start | bytes 1474560 | tf_op jit(solution)/shard_map/all_gather | solution.py:148
  11.6 98.1 %all-gather.9.cloned.1.call-start = ((), (), s32[]{:S(2)}) async-start(), calls=%async_computation.7 | async-start | bytes 1474560 | tf_op jit(solution)/shard_map/all_gather | solution.py:148
  18.1 139.4 %all-gather.11.cloned.1.call-start = ((), (), s32[]{:S(2)}) async-start(), calls=%async_computation.8 | async-start | bytes 1474560 | tf_op jit(solution)/shard_map/all_gather | solution.py:148
  59.7 28.7 %collective-permute-start.11 = (bf16[4,2,96,768]{3,2,1,0:T(8,128)(2,1)}, bf16[4,2,96,768]{3,2,1,0:T(8,128)(2,1)}, u32[]{:S(2)}, u32[]{:S(2)}) collective-permute-start(bf16[4,2,96,768]{3,2,1,0:T(8,128)(2,1)} %bitcast.35.refs_4_.refs_8_), channel_id=1, source_target_pairs={{0,4},{4,0},{8,12},{12,8},{16,20},{20,16},{24,28},{28,24},{1,5},{5... | collective-permute-start | bytes 3538952 | tf_op jit(solution)/shard_map/ppermute | solution.py:111
  61.2 28.4 %collective-permute-start.14 = (bf16[4,2,96,768]{3,2,1,0:T(8,128)(2,1)}, bf16[4,2,96,768]{3,2,1,0:T(8,128)(2,1)}, u32[]{:S(2)}, u32[]{:S(2)}) collective-permute-start(bf16[4,2,96,768]{3,2,1,0:T(8,128)(2,1)} %bitcast.35.refs_4_.refs_8_), channel_id=1, source_target_pairs={{0,2},{1,3},{2,0},{3,1},{4,6},{5,7},{6,4},{7,5},{8,10},{9,11},{10,... | collective-permute-start | bytes 3538952 | tf_op jit(solution)/shard_map/ppermute | solution.py:111
  76.6 33.1 %collective-permute-start.12 = (bf16[4,2,96,768]{3,2,1,0:T(8,128)(2,1)}, bf16[4,2,96,768]{3,2,1,0:T(8,128)(2,1)}, u32[]{:S(2)}, u32[]{:S(2)}) collective-permute-start(bf16[4,2,96,768]{3,2,1,0:T(8,128)(2,1)} %bitcast.35.refs_4_.refs_8_), channel_id=1, source_target_pairs={{0,1},{1,0},{2,3},{3,2},{4,5},{5,4},{6,7},{7,6},{8,9},{9,8},{10,11... | collective-permute-start | bytes 3538952 | tf_op jit(solution)/shard_map/ppermute | solution.py:111
  91.3 19.6 %collective-permute-start.13 = (bf16[4,2,96,768]{3,2,1,0:T(8,128)(2,1)}, bf16[4,2,96,768]{3,2,1,0:T(8,128)(2,1)}, u32[]{:S(2)}, u32[]{:S(2)}) collective-permute-start(bf16[4,2,96,768]{3,2,1,0:T(8,128)(2,1)} %collective-permute-done.11.refs_5_.refs_9_), channel_id=1, source_target_pairs={{0,1},{1,0},{2,3},{3,2},{4,5},{5,4},{6,7},{7,6},{8,9},{9,8},{10,11... | collective-permute-start | bytes 3538952 | tf_op jit(solution)/shard_map/ppermute | solution.py:111
  91.3 20.2 %collective-permute-start.16 = (bf16[4,2,96,768]{3,2,1,0:T(8,128)(2,1)}, bf16[4,2,96,768]{3,2,1,0:T(8,128)(2,1)}, u32[]{:S(2)}, u32[]{:S(2)}) collective-permute-start(bf16[4,2,96,768]{3,2,1,0:T(8,128)(2,1)} %collective-permute-done.14.refs_8_.refs_12_), channel_id=1, source_target_pairs={{0,1},{1,0},{2,3},{3,2},{4,5},{5,4},{6,7},{7,6},{8,9},{9,8},{10,11... | collective-permute-start | bytes 3538952 | tf_op jit(solution)/shard_map/ppermute | solution.py:111
  106.3 280.4 %reduce-scatter.6.cloned.1.call-start = ((), (), s32[]{:S(2)}) async-start(), calls=%async_computation.4 | async-start | bytes 1474560 | tf_op jit(solution)/shard_map/reduce_scatter | solution.py:202
  109.7 28.8 %collective-permute-start.18 = (bf16[4,2,96,768]{3,2,1,0:T(8,128)(2,1)}, bf16[4,2,96,768]{3,2,1,0:T(8,128)(2,1)}, u32[]{:S(2)}, u32[]{:S(2)}) collective-permute-start(bf16[4,2,96,768]{3,2,1,0:T(8,128)(2,1)} %bitcast.123), channel_id=1, source_target_pairs={{0,4},{4,0},{8,12},{12,8},{16,20},{20,16},{24,28},{28,24},{1,5},{5... | collective-permute-start | bytes 3538952 | tf_op jit(solution)/shard_map/ppermute | solution.py:111
  110.4 28.4 %collective-permute-start.21 = (bf16[4,2,96,768]{3,2,1,0:T(8,128)(2,1)}, bf16[4,2,96,768]{3,2,1,0:T(8,128)(2,1)}, u32[]{:S(2)}, u32[]{:S(2)}) collective-permute-start(bf16[4,2,96,768]{3,2,1,0:T(8,128)(2,1)} %bitcast.124), channel_id=1, source_target_pairs={{0,2},{1,3},{2,0},{3,1},{4,6},{5,7},{6,4},{7,5},{8,10},{9,11},{10,... | collective-permute-start | bytes 3538952 | tf_op jit(solution)/shard_map/ppermute | solution.py:111
  110.9 46.5 %collective-permute-start.19 = (bf16[4,2,96,768]{3,2,1,0:T(8,128)(2,1)}, bf16[4,2,96,768]{3,2,1,0:T(8,128)(2,1)}, u32[]{:S(2)}, u32[]{:S(2)}) collective-permute-start(bf16[4,2,96,768]{3,2,1,0:T(8,128)(2,1)} %bitcast.125), channel_id=1, source_target_pairs={{0,1},{1,0},{2,3},{3,2},{4,5},{5,4},{6,7},{7,6},{8,9},{9,8},{10,11... | collective-permute-start | bytes 3538952 | tf_op jit(solution)/shard_map/ppermute | solution.py:111
  157.5 28.7 %collective-permute-start.29 = (bf16[4,2,96,768]{3,2,1,0:T(8,128)(2,1)}, bf16[4,2,96,768]{3,2,1,0:T(8,128)(2,1)S(1)}, u32[]{:S(2)}, u32[]{:S(2)}) collective-permute-start(bf16[4,2,96,768]{3,2,1,0:T(8,128)(2,1)} %bitcast.128), channel_id=1, source_target_pairs={{0,4},{4,0},{8,12},{12,8},{16,20},{20,16},{24,28},{28,24},{1,5},{5... | collective-permute-start | bytes 3538952 | tf_op jit(solution)/shard_map/ppermute | solution.py:111
  159.0 28.3 %collective-permute-start.32 = (bf16[4,2,96,768]{3,2,1,0:T(8,128)(2,1)}, bf16[4,2,96,768]{3,2,1,0:T(8,128)(2,1)S(1)}, u32[]{:S(2)}, u32[]{:S(2)}) collective-permute-start(bf16[4,2,96,768]{3,2,1,0:T(8,128)(2,1)} %bitcast.129), channel_id=1, source_target_pairs={{0,2},{1,3},{2,0},{3,1},{4,6},{5,7},{6,4},{7,5},{8,10},{9,11},{10,... | collective-permute-start | bytes 3538952 | tf_op jit(solution)/shard_map/ppermute | solution.py:111
  188.8 21.5 %collective-permute-start.38 = (bf16[6,120,768]{2,1,0:T(8,128)(2,1)S(1)}, bf16[6,120,768]{2,1,0:T(8,128)(2,1)S(1)}, u32[]{:S(2)}, u32[]{:S(2)}) collective-permute-start(bf16[6,120,768]{2,1,0:T(8,128)(2,1)S(1)} %get-tuple-element.355), channel_id=1, source_target_pairs={{0,1},{1,0},{2,3},{3,2},{4,5},{5,4},{6,7},{7,6},{8,9},{9,8},{10,11... | collective-permute-start | bytes 3317768 | tf_op jit(solution)/shard_map/ppermute | solution.py:111
  189.5 23.5 %collective-permute-start.30 = (bf16[4,2,96,768]{3,2,1,0:T(8,128)(2,1)S(1)}, bf16[4,2,96,768]{3,2,1,0:T(8,128)(2,1)S(1)}, u32[]{:S(2)}, u32[]{:S(2)}) collective-permute-start(bf16[4,2,96,768]{3,2,1,0:T(8,128)(2,1)S(1)} %bitcast.130), channel_id=1, source_target_pairs={{0,1},{1,0},{2,3},{3,2},{4,5},{5,4},{6,7},{7,6},{8,9},{9,8},{10,11... | collective-permute-start | bytes 3538952 | tf_op jit(solution)/shard_map/ppermute | solution.py:111
  190.1 19.6 %collective-permute-start.36 = (bf16[4,1,96,768]{3,2,1,0:T(8,128)(2,1)S(1)}, bf16[4,1,96,768]{3,2,1,0:T(8,128)(2,1)S(1)}, u32[]{:S(2)}, u32[]{:S(2)}) collective-permute-start(bf16[4,1,96,768]{3,2,1,0:T(8,128)(2,1)S(1)} %slice.486), channel_id=1, source_target_pairs={{0,4},{4,0},{8,12},{12,8},{16,20},{20,16},{24,28},{28,24},{1,5},{5... | collective-permute-start | bytes 1769480 | tf_op jit(solution)/shard_map/ppermute | solution.py:111
  190.8 24.3 %collective-permute-start.31 = (bf16[4,2,96,768]{3,2,1,0:T(8,128)(2,1)S(1)}, bf16[4,2,96,768]{3,2,1,0:T(8,128)(2,1)S(1)}, u32[]{:S(2)}, u32[]{:S(2)}) collective-permute-start(bf16[4,2,96,768]{3,2,1,0:T(8,128)(2,1)S(1)} %collective-permute-done.29.refs_5_.refs_13_), channel_id=1, source_target_pairs={{0,1},{1,0},{2,3},{3,2},{4,5},{5,4},{6,7},{7,6},{8,9},{9,8},{10,11... | collective-permute-start | bytes 3538952 | tf_op jit(solution)/shard_map/ppermute | solution.py:111
  240.6 28.8 %collective-permute-start.44 = (bf16[2,384,768]{2,1,0:T(8,128)(2,1)S(1)}, bf16[2,384,768]{2,1,0:T(8,128)(2,1)S(1)}, u32[]{:S(2)}, u32[]{:S(2)}) collective-permute-start(bf16[2,384,768]{2,1,0:T(8,128)(2,1)S(1)} %get-tuple-element.375.refs_16_), channel_id=1, source_target_pairs={{0,4},{4,0},{8,12},{12,8},{16,20},{20,16},{24,28},{28,24},{1,5},{5... | collective-permute-start | bytes 3538952 | tf_op jit(solution)/shard_map/ppermute | solution.py:111
  241.2 28.8 %collective-permute-start.45 = (bf16[2,384,768]{2,1,0:T(8,128)(2,1)S(1)}, bf16[2,384,768]{2,1,0:T(8,128)(2,1)S(1)}, u32[]{:S(2)}, u32[]{:S(2)}) collective-permute-start(bf16[2,384,768]{2,1,0:T(8,128)(2,1)S(1)} %get-tuple-element.398), channel_id=1, source_target_pairs={{0,2},{1,3},{2,0},{3,1},{4,6},{5,7},{6,4},{7,5},{8,10},{9,11},{10,... | collective-permute-start | bytes 3538952 | tf_op jit(solution)/shard_map/ppermute | solution.py:111
  252.9 43.3 %collective-permute-start.48 = (bf16[384,768]{1,0:T(8,128)(2,1)}, bf16[384,768]{1,0:T(8,128)(2,1)}, u32[]{:S(2)}, u32[]{:S(2)}) collective-permute-start(bf16[384,768]{1,0:T(8,128)(2,1)} %get-tuple-element.415), channel_id=1, source_target_pairs={{0,2},{1,3},{2,0},{3,1},{4,6},{5,7},{6,4},{7,5},{8,10},{9,11},{10,... | collective-permute-start | bytes 1769480 | tf_op jit(solution)/shard_map/ppermute | solution.py:111
  254.3 41.9 %collective-permute-start.49 = (bf16[384,768]{1,0:T(8,128)(2,1)}, bf16[384,768]{1,0:T(8,128)(2,1)}, u32[]{:S(2)}, u32[]{:S(2)}) collective-permute-start(bf16[384,768]{1,0:T(8,128)(2,1)} %get-tuple-element.416), channel_id=1, source_target_pairs={{0,4},{4,0},{8,12},{12,8},{16,20},{20,16},{24,28},{28,24},{1,5},{5... | collective-permute-start | bytes 1769480 | tf_op jit(solution)/shard_map/ppermute | solution.py:111
  255.7 45.4 %collective-permute-start.46 = (bf16[384,768]{1,0:T(8,128)(2,1)}, bf16[384,768]{1,0:T(8,128)(2,1)}, u32[]{:S(2)}, u32[]{:S(2)}) collective-permute-start(bf16[384,768]{1,0:T(8,128)(2,1)} %get-tuple-element.408), channel_id=1, source_target_pairs={{0,2},{1,3},{2,0},{3,1},{4,6},{5,7},{6,4},{7,5},{8,10},{9,11},{10,... | collective-permute-start | bytes 1769480 | tf_op jit(solution)/shard_map/ppermute | solution.py:111
  269.4 31.7 %collective-permute-start.47 = (bf16[384,768]{1,0:T(8,128)(2,1)}, bf16[384,768]{1,0:T(8,128)(2,1)}, u32[]{:S(2)}, u32[]{:S(2)}) collective-permute-start(bf16[384,768]{1,0:T(8,128)(2,1)} %get-tuple-element.409), channel_id=1, source_target_pairs={{0,4},{4,0},{8,12},{12,8},{16,20},{20,16},{24,28},{28,24},{1,5},{5... | collective-permute-start | bytes 1769480 | tf_op jit(solution)/shard_map/ppermute | solution.py:111
  304.1 104.1 %reduce-scatter.4.cloned.1.call-start = ((), (), s32[]{:S(2)}) async-start(), calls=%async_computation.3 | async-start | bytes 1474560 | tf_op jit(solution)/shard_map/reduce_scatter | solution.py:202
  304.1 28.8 %collective-permute-start.51 = (bf16[2,384,768]{2,1,0:T(8,128)(2,1)}, bf16[2,384,768]{2,1,0:T(8,128)(2,1)}, u32[]{:S(2)}, u32[]{:S(2)}) collective-permute-start(bf16[2,384,768]{2,1,0:T(8,128)(2,1)} %copy-done.32), channel_id=1, source_target_pairs={{0,4},{4,0},{8,12},{12,8},{16,20},{20,16},{24,28},{28,24},{1,5},{5... | collective-permute-start | bytes 3538952 | tf_op jit(solution)/shard_map/ppermute | solution.py:111
  305.6 28.4 %collective-permute-start.52 = (bf16[2,384,768]{2,1,0:T(8,128)(2,1)}, bf16[2,384,768]{2,1,0:T(8,128)(2,1)}, u32[]{:S(2)}, u32[]{:S(2)}) collective-permute-start(bf16[2,384,768]{2,1,0:T(8,128)(2,1)} %copy-done.31), channel_id=1, source_target_pairs={{0,2},{1,3},{2,0},{3,1},{4,6},{5,7},{6,4},{7,5},{8,10},{9,11},{10,... | collective-permute-start | bytes 3538952 | tf_op jit(solution)/shard_map/ppermute | solution.py:111
  337.3 91.3 %reduce-scatter.8.cloned.1.call-start = ((), (), s32[]{:S(2)}) async-start(), calls=%async_computation.5 | async-start | bytes 1474560 | tf_op jit(solution)/shard_map/reduce_scatter | solution.py:202
  337.7 27.4 %collective-permute-start.60 = (bf16[2,384,768]{2,1,0:T(8,128)(2,1)S(1)}, bf16[2,384,768]{2,1,0:T(8,128)(2,1)}, u32[]{:S(2)}, u32[]{:S(2)}) collective-permute-start(bf16[2,384,768]{2,1,0:T(8,128)(2,1)S(1)} %copy-done.30), channel_id=1, source_target_pairs={{0,4},{4,0},{8,12},{12,8},{16,20},{20,16},{24,28},{28,24},{1,5},{5... | collective-permute-start | bytes 3538952 | tf_op jit(solution)/shard_map/ppermute | solution.py:111
  338.5 27.4 %collective-permute-start.61 = (bf16[2,384,768]{2,1,0:T(8,128)(2,1)S(1)}, bf16[2,384,768]{2,1,0:T(8,128)(2,1)}, u32[]{:S(2)}, u32[]{:S(2)}) collective-permute-start(bf16[2,384,768]{2,1,0:T(8,128)(2,1)S(1)} %copy-done.27), channel_id=1, source_target_pairs={{0,2},{1,3},{2,0},{3,1},{4,6},{5,7},{6,4},{7,5},{8,10},{9,11},{10,... | collective-permute-start | bytes 3538952 | tf_op jit(solution)/shard_map/ppermute | solution.py:111
  370.1 29.0 %collective-permute-start.53 = (bf16[384,384]{1,0:T(8,128)(2,1)}, bf16[384,384]{1,0:T(8,128)(2,1)}, u32[]{:S(2)}, u32[]{:S(2)}) collective-permute-start(bf16[384,384]{1,0:T(8,128)(2,1)} %get-tuple-element.440), channel_id=1, source_target_pairs={{0,2},{1,3},{2,0},{3,1},{4,6},{5,7},{6,4},{7,5},{8,10},{9,11},{10,... | collective-permute-start | bytes 884744 | tf_op jit(solution)/shard_map/ppermute | solution.py:111
  370.8 28.4 %collective-permute-start.54 = (bf16[384,384]{1,0:T(8,128)(2,1)}, bf16[384,384]{1,0:T(8,128)(2,1)}, u32[]{:S(2)}, u32[]{:S(2)}) collective-permute-start(bf16[384,384]{1,0:T(8,128)(2,1)} %get-tuple-element.441), channel_id=1, source_target_pairs={{0,4},{4,0},{8,12},{12,8},{16,20},{20,16},{24,28},{28,24},{1,5},{5... | collective-permute-start | bytes 884744 | tf_op jit(solution)/shard_map/ppermute | solution.py:111
  (154 other events, 1312.2 us)
Sparse Core Ops, SparseCore 0:
  11.7 38.0 all-gather.6
  52.0 30.5 all-gather.8
  106.4 36.8 all-gather.10
  304.2 36.1 reduce-scatter.5
  342.6 30.2 reduce-scatter.3
  375.0 34.4 reduce-scatter.7
